TPU v7x, 32 devices: a whole 2x2x4 slice. The times are simulated.
32 devices in a mesh: blk: 2 (over x), dp: 16 (over z, y, core).
Axes of the slice: x: 2, y: 2, z: 4, core: 2. Of those that a mesh axis runs over, the one named last changes fastest.
Arguments:
- hidden: bfloat16 [16, 4096, 768], P('dp', 'blk'), may hold values from -6 to 6
- separators: int32 [16], P('dp'), may hold values from 1 to 4095, as said below
- out_grad: bfloat16 [16, 4096, 768], P('dp', 'blk'), may hold values from -6 to 6
- w_query: float32 [768, 384], P('dp'), may hold values from -0.21875 to 0.21875
- b_query: float32 [384], P('dp'), may hold values from -2 to 2
- w_key: float32 [768, 384], P('dp'), may hold values from -0.21875 to 0.21875
- w_value: float32 [768, 384], P('dp'), may hold values from -0.21875 to 0.21875
- b_value: float32 [384], P('dp'), may hold values from -2 to 2
- depth_kernel: float32 [768, 9], P('dp'), may hold values from -2 to 2
- w_point: float32 [768, 384], P('dp'), may hold values from -0.21875 to 0.21875
- b_keyconv: float32 [384], P('dp'), may hold values from -2 to 2
- w_kernel: float32 [384, 54], P('dp'), may hold values from -0.3125 to 0.3125
- kernel_bias: float32 [54], replicated, may hold values from -3 to 3
- w_convout: float32 [768, 384], P('dp'), may hold values from -0.21875 to 0.21875
- b_convout: float32 [384], P('dp'), may hold values from -2 to 2
- w_dense: float32 [768, 768], P('dp'), may hold values from -0.3125 to 0.3125
- b_dense: float32 [768], P('dp'), may hold values from -2 to 2
- gain_attn: float32 [768], P('dp'), may hold values from 0.5 to 1.5
- shift_attn: float32 [768], P('dp'), may hold values from -2 to 2
- w_up: float32 [2, 384, 1536], P(None, 'dp'), may hold values from -0.3125 to 0.3125
- b_up: float32 [3072], P('dp'), may hold values from -2 to 2
- w_down: float32 [2, 1536, 384], P(None, 'dp'), may hold values from -0.15625 to 0.15625
- b_down: float32 [768], P('dp'), may hold values from -2 to 2
- gain_out: float32 [768], P('dp'), may hold values from 0.5 to 1.5
- shift_out: float32 [768], P('dp'), may hold values from -2 to 2
Outputs:
- output: bfloat16 [16, 4096, 768], P('dp', 'blk')
- grad_hidden: bfloat16 [16, 4096, 768], P('dp', 'blk')
- grad_w_query: float32 [768, 384], P('dp')
- grad_b_query: float32 [384], P('dp')
- grad_w_key: float32 [768, 384], P('dp')
- grad_w_value: float32 [768, 384], P('dp')
- grad_b_value: float32 [384], P('dp')
- grad_depth_kernel: float32 [768, 9], P('dp')
- grad_w_point: float32 [768, 384], P('dp')
- grad_b_keyconv: float32 [384], P('dp')
- grad_w_kernel: float32 [384, 54], P('dp')
- grad_kernel_bias: float32 [54], replicated
- grad_w_convout: float32 [768, 384], P('dp')
- grad_b_convout: float32 [384], P('dp')
- grad_w_dense: float32 [768, 768], P('dp')
- grad_b_dense: float32 [768], P('dp')
- grad_gain_attn: float32 [768], P('dp')
- grad_shift_attn: float32 [768], P('dp')
- grad_w_up: float32 [2, 384, 1536], P(None, 'dp')
- grad_b_up: float32 [3072], P('dp')
- grad_w_down: float32 [2, 1536, 384], P(None, 'dp')
- grad_b_down: float32 [768], P('dp')
- grad_gain_out: float32 [768], P('dp')
- grad_shift_out: float32 [768], P('dp')
Inputs may be any that keep to these rules, and one draw needn't show every extreme that they name: Each row's second segment starts at its separator, so both segments are nonempty. Either all even rows or all odd rows, which ones drawn from the seed, have their separator below 2048 or above 2048; the other rows' separators may lie anywhere.
All inputs are finite; a program needn't handle non-finite values.
Results may differ from a plain program's by a relative error of at most 0.034.
Values may be sent and summed in bfloat16 or wider, within the bound.
A program may use at most 256 MiB of HBM per device.

v0:
```python
from functools import partial
import math

import jax
import jax.numpy as jnp
from jax import lax
from jax.sharding import PartitionSpec as P

HEADS = 6
HD = 64
KSIZE = 9
ATT = 384


EPS = 1e-12
NEGATIVE = -1e30


def with_halo(cells, sides, width):
    for axis, dim in sides:
        count = lax.axis_size(axis)
        ends = count - 1
        head = lax.slice_in_dim(cells, 0, width, axis=dim)
        tail = lax.slice_in_dim(cells, cells.shape[dim] - width, cells.shape[dim], axis=dim)
        cells = jnp.concatenate(
            [
                lax.ppermute(tail, axis, [(i, (i + 1) % count) for i in range(ends)]),
                cells,
                lax.ppermute(head, axis, [((i + 1) % count, i) for i in range(ends)]),
            ],
            axis=dim,
        )
    return cells


def for_sending(value):

    def short(part):
        return part.astype(jnp.bfloat16) if part.dtype == jnp.float32 else part

    return jax.tree.map(short, value)


def product(left, right):
    return jnp.dot(left, right, preferred_element_type=jnp.float32)


def outer_sum(left, right):
    return lax.dot_general(
        left, right, (((0,), (0,)), ((), ())), preferred_element_type=jnp.float32
    )


def back_product(left, right):
    return lax.dot_general(
        left, right, (((1,), (1,)), ((), ())), preferred_element_type=jnp.float32
    )


def column_sum(values):
    return jnp.sum(values.astype(jnp.float32), axis=0)


def grouped(inputs, weight):
    groups, inner, outer = weight.shape
    parts = inputs.reshape(inputs.shape[0], groups, inner)
    mixed = jnp.einsum("ngi,gio->ngo", parts, weight, preferred_element_type=jnp.float32)
    return mixed.reshape(inputs.shape[0], groups * outer)


def grouped_back(inputs, weight, grad_out):
    groups, inner, outer = weight.shape
    count = inputs.shape[0]
    parts = inputs.reshape(count, groups, inner)
    grads = grad_out.reshape(count, groups, outer)
    grad_in = jnp.einsum("ngo,gio->ngi", grads, weight, preferred_element_type=jnp.float32)
    grad_weight = jnp.einsum("ngi,ngo->gio", parts, grads, preferred_element_type=jnp.float32)
    return (grad_in.reshape(count, groups * inner), grad_weight)


def layer_norm(values, gain, shift):
    centre = values - jnp.mean(values, axis=-1, keepdims=True)
    spread = jnp.mean(centre * centre, axis=-1, keepdims=True)
    return centre * lax.rsqrt(spread + EPS) * gain + shift


def gelu_exact(values):
    return jax.nn.gelu(values, approximate=False)


def depth_conv(kernel, padded):
    length = padded.shape[1] - kernel.shape[1] + 1
    return sum((padded[:, tap : tap + length] * kernel[:, tap] for tap in range(kernel.shape[1])))


def span_conv(kernel, padded):
    length = kernel.shape[1]
    return sum(
        (
            kernel[:, :, :, tap, None] * padded[:, tap : tap + length]
            for tap in range(kernel.shape[3])
        )
    )


def over_blocks(step, carry, parts):
    row_count, count = (parts[0].shape[0], parts[0].shape[1])
    size = math.gcd(count, 512)
    blocks = count // size
    split = tuple(
        (part.reshape((row_count, blocks, size) + part.shape[2:]).swapaxes(0, 1) for part in parts)
    )
    starts = size * jnp.arange(blocks, dtype=jnp.int32)

    def visit(state, item):
        return (step(state, item[0], item[1]), None)

    carry, unused = lax.scan(visit, carry, (split, starts))
    return carry


def local(
    hidden,
    separators,
    out_grad,
    w_query,
    b_query,
    w_key,
    w_value,
    b_value,
    depth_kernel,
    w_point,
    b_keyconv,
    w_kernel,
    kernel_bias,
    w_convout,
    b_convout,
    w_dense,
    b_dense,
    gain_attn,
    shift_attn,
    w_up,
    b_up,
    w_down,
    b_down,
    gain_out,
    shift_out,
):
    shards = [
        master.astype(jnp.bfloat16)
        for master in (
            w_query,
            b_query,
            w_key,
            w_value,
            b_value,
            depth_kernel,
            w_point,
            b_keyconv,
            w_kernel,
            w_convout,
            b_convout,
            w_dense,
            b_dense,
            gain_attn,
            shift_attn,
            w_up,
            b_up,
            w_down,
            b_down,
            gain_out,
            shift_out,
        )
    ]
    weights = (
        lax.all_gather(shards[0], "dp", axis=0, tiled=True),
        lax.all_gather(shards[1], "dp", axis=0, tiled=True),
        lax.all_gather(shards[2], "dp", axis=0, tiled=True),
        lax.all_gather(shards[3], "dp", axis=0, tiled=True),
        lax.all_gather(shards[4], "dp", axis=0, tiled=True),
        lax.all_gather(shards[5], "dp", axis=0, tiled=True),
        lax.all_gather(shards[6], "dp", axis=0, tiled=True),
        lax.all_gather(shards[7], "dp", axis=0, tiled=True),
        lax.all_gather(shards[8], "dp", axis=0, tiled=True),
        lax.all_gather(shards[9], "dp", axis=0, tiled=True),
        lax.all_gather(shards[10], "dp", axis=0, tiled=True),
        lax.all_gather(shards[11], "dp", axis=0, tiled=True),
        lax.all_gather(shards[12], "dp", axis=0, tiled=True),
        lax.all_gather(shards[13], "dp", axis=0, tiled=True),
        lax.all_gather(shards[14], "dp", axis=0, tiled=True),
        lax.all_gather(shards[15], "dp", axis=1, tiled=True),
        lax.all_gather(shards[16], "dp", axis=0, tiled=True),
        lax.all_gather(shards[17], "dp", axis=1, tiled=True),
        lax.all_gather(shards[18], "dp", axis=0, tiled=True),
        lax.all_gather(shards[19], "dp", axis=0, tiled=True),
        lax.all_gather(shards[20], "dp", axis=0, tiled=True),
    )
    (
        wt_query,
        bias_query,
        wt_key,
        wt_value,
        bias_value,
        wt_depth,
        wt_point,
        bias_keyconv,
        wt_kernel,
        wt_convout,
        bias_convout,
        wt_dense,
        bias_dense,
        gain_one,
        shift_one,
        wt_up,
        bias_up,
        wt_down,
        bias_down,
        gain_two,
        shift_two,
    ) = weights
    row_count, span, width = hidden.shape
    tokens = row_count * span
    reach = KSIZE // 2
    full_length = span * lax.axis_size("blk")
    flat = hidden.reshape(tokens, width)
    query_low = (product(flat, wt_query) + bias_query).astype(jnp.bfloat16)
    key_low = product(flat, wt_key).astype(jnp.bfloat16).reshape(row_count, span, ATT)
    value_low = (
        (product(flat, wt_value) + bias_value).astype(jnp.bfloat16).reshape(row_count, span, ATT)
    )
    padded = with_halo(hidden, (("blk", 1),), reach)
    padded_pos = (
        lax.axis_index("blk") * span - reach + jnp.arange(span + 2 * reach, dtype=jnp.int32)
    )
    inside = ((padded_pos >= 0) & (padded_pos < full_length)).astype(jnp.float32)
    conv_values = product(padded.reshape(-1, width), wt_convout) + bias_convout
    conv_values = (
        conv_values.reshape(row_count, span + 2 * reach, ATT) * inside[None, :, None]
    ).astype(jnp.bfloat16)
    conv_heads = conv_values.astype(jnp.float32).reshape(row_count, span + 2 * reach, HEADS, HD)
    depth, depth_pull = jax.vjp(
        depth_conv, wt_depth.astype(jnp.float32), padded.astype(jnp.float32)
    )
    depth_low = depth.astype(jnp.bfloat16).reshape(tokens, width)
    keyconv = product(depth_low, wt_point) + bias_keyconv
    attn_key = (keyconv * query_low.astype(jnp.float32)).astype(jnp.bfloat16)
    logits = (product(attn_key, wt_kernel) + kernel_bias).reshape(row_count, span, HEADS, KSIZE)
    kernel, soft_pull = jax.vjp(partial(jax.nn.softmax, axis=-1), logits)
    conv, conv_pull = jax.vjp(span_conv, kernel, conv_heads)
    position = lax.axis_index("blk") * span + jnp.arange(span, dtype=jnp.int32)
    query_seg = position[None, :] >= separators[:, None]
    query_heads = query_low.reshape(row_count, span, HEADS, HD)
    scale = float(HD) ** (-0.5)

    def scored(keys, first):
        size = keys.shape[1]
        key_heads = keys.reshape(row_count, size, HEADS, HD)
        raw = (
            jnp.einsum(
                "rqhd,rkhd->rhqk", query_heads, key_heads, preferred_element_type=jnp.float32
            )
            * scale
        )
        key_seg = (first + jnp.arange(size, dtype=jnp.int32))[None, :] >= separators[:, None]
        same = (query_seg[:, :, None] == key_seg[:, None, :])[:, None]
        return (jnp.where(same, raw, NEGATIVE), same, key_heads)

    def forward_step(state, block, first):
        best, total, accum = state
        keys, values = block
        scores, same, key_heads = scored(keys, first)
        value_heads = values.reshape(key_heads.shape)
        newest = jnp.maximum(best, jnp.max(scores, axis=-1))
        factor = jnp.exp(best - newest)
        weights_now = jnp.where(same, jnp.exp(scores - newest[..., None]), 0.0)
        total = total * factor + jnp.sum(weights_now, axis=-1)
        accum = accum * factor[..., None] + jnp.einsum(
            "rhqk,rkhd->rhqd",
            weights_now.astype(jnp.bfloat16),
            value_heads,
            preferred_element_type=jnp.float32,
        )
        return (newest, total, accum)

    start_state = (
        jnp.full((row_count, HEADS, span), NEGATIVE, jnp.float32),
        jnp.zeros((row_count, HEADS, span), jnp.float32),
        jnp.zeros((row_count, HEADS, span, HD), jnp.float32),
    )
    best, total, accum = over_blocks(
        forward_step,
        start_state,
        (
            lax.all_gather(key_low, "blk", axis=1, tiled=True),
            lax.all_gather(value_low, "blk", axis=1, tiled=True),
        ),
    )
    log_total = best + jnp.log(total)
    out_heads = accum / total[..., None]
    attended = out_heads.transpose(0, 2, 1, 3).reshape(tokens, ATT)
    context = jnp.concatenate([attended, conv.reshape(tokens, ATT)], axis=-1).astype(jnp.bfloat16)
    dense = product(context, wt_dense) + bias_dense
    normed, first_pull = jax.vjp(
        layer_norm,
        dense + flat.astype(jnp.float32),
        gain_one.astype(jnp.float32),
        shift_one.astype(jnp.float32),
    )
    normed_low = normed.astype(jnp.bfloat16)
    upward = grouped(normed_low, wt_up) + bias_up
    activated, gelu_pull = jax.vjp(gelu_exact, upward)
    activated_low = activated.astype(jnp.bfloat16)
    downward = grouped(activated_low, wt_down) + bias_down
    output, second_pull = jax.vjp(
        layer_norm, downward + normed, gain_two.astype(jnp.float32), shift_two.astype(jnp.float32)
    )
    weights = (
        lax.all_gather(shards[0], "dp", axis=0, tiled=True),
        lax.all_gather(shards[1], "dp", axis=0, tiled=True),
        lax.all_gather(shards[2], "dp", axis=0, tiled=True),
        lax.all_gather(shards[3], "dp", axis=0, tiled=True),
        lax.all_gather(shards[4], "dp", axis=0, tiled=True),
        lax.all_gather(shards[5], "dp", axis=0, tiled=True),
        lax.all_gather(shards[6], "dp", axis=0, tiled=True),
        lax.all_gather(shards[7], "dp", axis=0, tiled=True),
        lax.all_gather(shards[8], "dp", axis=0, tiled=True),
        lax.all_gather(shards[9], "dp", axis=0, tiled=True),
        lax.all_gather(shards[10], "dp", axis=0, tiled=True),
        lax.all_gather(shards[11], "dp", axis=0, tiled=True),
        lax.all_gather(shards[12], "dp", axis=0, tiled=True),
        lax.all_gather(shards[13], "dp", axis=0, tiled=True),
        lax.all_gather(shards[14], "dp", axis=0, tiled=True),
        lax.all_gather(shards[15], "dp", axis=1, tiled=True),
        lax.all_gather(shards[16], "dp", axis=0, tiled=True),
        lax.all_gather(shards[17], "dp", axis=1, tiled=True),
        lax.all_gather(shards[18], "dp", axis=0, tiled=True),
        lax.all_gather(shards[19], "dp", axis=0, tiled=True),
        lax.all_gather(shards[20], "dp", axis=0, tiled=True),
    )
    (
        wt_query,
        bias_query,
        wt_key,
        wt_value,
        bias_value,
        wt_depth,
        wt_point,
        bias_keyconv,
        wt_kernel,
        wt_convout,
        bias_convout,
        wt_dense,
        bias_dense,
        gain_one,
        shift_one,
        wt_up,
        bias_up,
        wt_down,
        bias_down,
        gain_two,
        shift_two,
    ) = weights
    grad_sum_two, grad_gain_out, grad_shift_out = second_pull(
        out_grad.reshape(tokens, width).astype(jnp.float32)
    )
    grad_down = grad_sum_two.astype(jnp.bfloat16)
    grad_b_down = column_sum(grad_down)
    grad_act, grad_w_down = grouped_back(activated_low, wt_down, grad_down)
    grad_upward = gelu_pull(grad_act)[0].astype(jnp.bfloat16)
    grad_b_up = column_sum(grad_upward)
    grad_normed_up, grad_w_up = grouped_back(normed_low, wt_up, grad_upward)
    grad_sum_one, grad_gain_attn, grad_shift_attn = first_pull(grad_sum_two + grad_normed_up)
    grad_dense = grad_sum_one.astype(jnp.bfloat16)
    grad_b_dense = column_sum(grad_dense)
    grad_w_dense = outer_sum(context, grad_dense)
    grad_context = back_product(grad_dense, wt_dense).astype(jnp.bfloat16)
    grad_attended = grad_context[:, :ATT]
    grad_conv = grad_context[:, ATT:]
    grad_kernel, grad_conv_heads = conv_pull(
        grad_conv.astype(jnp.float32).reshape(row_count, span, HEADS, HD)
    )
    grad_logits = soft_pull(grad_kernel)[0].reshape(tokens, HEADS * KSIZE).astype(jnp.bfloat16)
    grad_kernel_bias = column_sum(grad_logits)
    grad_w_kernel = outer_sum(attn_key, grad_logits)
    grad_attn_key = back_product(grad_logits, wt_kernel).astype(jnp.bfloat16).astype(jnp.float32)
    grad_keyconv = (grad_attn_key * query_low.astype(jnp.float32)).astype(jnp.bfloat16)
    grad_query_conv = grad_attn_key * keyconv
    grad_b_keyconv = column_sum(grad_keyconv)
    grad_w_point = outer_sum(depth_low, grad_keyconv)
    grad_depth = back_product(grad_keyconv, wt_point).astype(jnp.bfloat16)
    grad_depth_kernel, grad_padded = depth_pull(
        grad_depth.astype(jnp.float32).reshape(row_count, span, width)
    )
    grad_view = grad_attended.reshape(row_count, span, HEADS, HD)
    delta = jnp.sum(
        grad_view.astype(jnp.float32) * out_heads.transpose(0, 2, 1, 3), axis=-1
    ).transpose(0, 2, 1)

    def backward_step(state, block, first):
        grad_query_sum, key_sums, value_sums = state
        keys, values = block
        scores, same, key_heads = scored(keys, first)
        value_heads = values.reshape(key_heads.shape)
        probs = jnp.where(same, jnp.exp(scores - log_total[..., None]), 0.0)
        grad_probs = jnp.einsum(
            "rqhd,rkhd->rhqk", grad_view, value_heads, preferred_element_type=jnp.float32
        )
        grad_scores = (probs * (grad_probs - delta[..., None])).astype(jnp.bfloat16)
        grad_query_sum = (
            grad_query_sum
            + jnp.einsum(
                "rhqk,rkhd->rqhd", grad_scores, key_heads, preferred_element_type=jnp.float32
            )
            * scale
        )
        grad_keys = (
            jnp.einsum(
                "rhqk,rqhd->rkhd", grad_scores, query_heads, preferred_element_type=jnp.float32
            )
            * scale
        )
        grad_values = jnp.einsum(
            "rhqk,rqhd->rkhd",
            probs.astype(jnp.bfloat16),
            grad_view,
            preferred_element_type=jnp.float32,
        )
        size = keys.shape[1]
        key_sums = lax.dynamic_update_slice_in_dim(
            key_sums, grad_keys.reshape(row_count, size, ATT), first, 1
        )
        value_sums = lax.dynamic_update_slice_in_dim(
            value_sums, grad_values.reshape(row_count, size, ATT), first, 1
        )
        return (grad_query_sum, key_sums, value_sums)

    back_state = (
        jnp.zeros((row_count, span, HEADS, HD), jnp.float32),
        jnp.zeros((row_count, full_length, ATT), jnp.float32),
        jnp.zeros((row_count, full_length, ATT), jnp.float32),
    )
    grad_query_attn, key_sums, value_sums = over_blocks(
        backward_step,
        back_state,
        (
            lax.all_gather(key_low, "blk", axis=1, tiled=True),
            lax.all_gather(value_low, "blk", axis=1, tiled=True),
        ),
    )
    grad_key_own, grad_value_own = (
        lax.psum_scatter(
            key_sums.astype(jnp.bfloat16), "blk", scatter_dimension=1, tiled=True
        ).astype(jnp.float32),
        lax.psum_scatter(
            value_sums.astype(jnp.bfloat16), "blk", scatter_dimension=1, tiled=True
        ).astype(jnp.float32),
    )
    grad_key = grad_key_own.reshape(tokens, ATT).astype(jnp.bfloat16)
    grad_value = grad_value_own.reshape(tokens, ATT).astype(jnp.bfloat16)
    grad_query = (grad_query_attn.reshape(tokens, ATT) + grad_query_conv).astype(jnp.bfloat16)
    grad_conv_pad = grad_conv_heads.reshape(row_count, span + 2 * reach, ATT)
    rim_lower = jnp.concatenate([grad_padded[:, :reach], grad_conv_pad[:, :reach]], axis=-1)
    rim_upper = jnp.concatenate(
        [grad_padded[:, span + reach :], grad_conv_pad[:, span + reach :]], axis=-1
    )
    incoming = with_halo(
        for_sending(jnp.concatenate([rim_lower, rim_upper], axis=1)), (("blk", 1),), reach
    )
    from_lower = incoming[:, :reach]
    from_upper = incoming[:, 3 * reach :]
    own_tokens = grad_padded[:, reach : span + reach].at[:, :reach].add(from_lower[..., :width])
    own_tokens = own_tokens.at[:, span - reach :].add(from_upper[..., :width])
    own_conv = grad_conv_pad[:, reach : span + reach].at[:, :reach].add(from_lower[..., width:])
    own_conv = own_conv.at[:, span - reach :].add(from_upper[..., width:])
    grad_convout = own_conv.reshape(tokens, ATT).astype(jnp.bfloat16)
    grad_w_query = outer_sum(flat, grad_query)
    grad_b_query = column_sum(grad_query)
    grad_w_key = outer_sum(flat, grad_key)
    grad_w_value = outer_sum(flat, grad_value)
    grad_b_value = column_sum(grad_value)
    grad_w_convout = outer_sum(flat, grad_convout)
    grad_b_convout = column_sum(grad_convout)
    grad_flat = (
        grad_sum_one
        + back_product(grad_query, wt_query)
        + back_product(grad_key, wt_key)
        + back_product(grad_value, wt_value)
        + back_product(grad_convout, wt_convout)
        + own_tokens.reshape(tokens, width)
    )
    grad_hidden = grad_flat.astype(jnp.bfloat16).reshape(row_count, span, width)
    summed = (
        lax.psum(grad_w_query.astype(jnp.bfloat16), "blk").astype(jnp.float32),
        lax.psum(grad_b_query.astype(jnp.bfloat16), "blk").astype(jnp.float32),
        lax.psum(grad_w_key.astype(jnp.bfloat16), "blk").astype(jnp.float32),
        lax.psum(grad_w_value.astype(jnp.bfloat16), "blk").astype(jnp.float32),
        lax.psum(grad_b_value.astype(jnp.bfloat16), "blk").astype(jnp.float32),
        lax.psum(grad_depth_kernel.astype(jnp.bfloat16), "blk").astype(jnp.float32),
        lax.psum(grad_w_point.astype(jnp.bfloat16), "blk").astype(jnp.float32),
        lax.psum(grad_b_keyconv.astype(jnp.bfloat16), "blk").astype(jnp.float32),
        lax.psum(grad_w_kernel.astype(jnp.bfloat16), "blk").astype(jnp.float32),
        lax.psum(grad_w_convout.astype(jnp.bfloat16), "blk").astype(jnp.float32),
        lax.psum(grad_b_convout.astype(jnp.bfloat16), "blk").astype(jnp.float32),
        lax.psum(grad_w_dense.astype(jnp.bfloat16), "blk").astype(jnp.float32),
        lax.psum(grad_b_dense.astype(jnp.bfloat16), "blk").astype(jnp.float32),
        lax.psum(grad_gain_attn.astype(jnp.bfloat16), "blk").astype(jnp.float32),
        lax.psum(grad_shift_attn.astype(jnp.bfloat16), "blk").astype(jnp.float32),
        lax.psum(grad_w_up.astype(jnp.bfloat16), "blk").astype(jnp.float32),
        lax.psum(grad_b_up.astype(jnp.bfloat16), "blk").astype(jnp.float32),
        lax.psum(grad_w_down.astype(jnp.bfloat16), "blk").astype(jnp.float32),
        lax.psum(grad_b_down.astype(jnp.bfloat16), "blk").astype(jnp.float32),
        lax.psum(grad_gain_out.astype(jnp.bfloat16), "blk").astype(jnp.float32),
        lax.psum(grad_shift_out.astype(jnp.bfloat16), "blk").astype(jnp.float32),
        lax.psum(grad_kernel_bias.astype(jnp.bfloat16), "blk").astype(jnp.float32),
    )
    tiled = jnp.broadcast_to(summed[21][None], (lax.axis_size("dp"), summed[21].shape[0]))
    shares = (
        lax.psum_scatter(
            summed[0].astype(jnp.bfloat16), "dp", scatter_dimension=0, tiled=True
        ).astype(jnp.float32),
        lax.psum_scatter(
            summed[1].astype(jnp.bfloat16), "dp", scatter_dimension=0, tiled=True
        ).astype(jnp.float32),
        lax.psum_scatter(
            summed[2].astype(jnp.bfloat16), "dp", scatter_dimension=0, tiled=True
        ).astype(jnp.float32),
        lax.psum_scatter(
            summed[3].astype(jnp.bfloat16), "dp", scatter_dimension=0, tiled=True
        ).astype(jnp.float32),
        lax.psum_scatter(
            summed[4].astype(jnp.bfloat16), "dp", scatter_dimension=0, tiled=True
        ).astype(jnp.float32),
        lax.psum_scatter(
            summed[5].astype(jnp.bfloat16), "dp", scatter_dimension=0, tiled=True
        ).astype(jnp.float32),
        lax.psum_scatter(
            summed[6].astype(jnp.bfloat16), "dp", scatter_dimension=0, tiled=True
        ).astype(jnp.float32),
        lax.psum_scatter(
            summed[7].astype(jnp.bfloat16), "dp", scatter_dimension=0, tiled=True
        ).astype(jnp.float32),
        lax.psum_scatter(
            summed[8].astype(jnp.bfloat16), "dp", scatter_dimension=0, tiled=True
        ).astype(jnp.float32),
        lax.psum_scatter(
            summed[9].astype(jnp.bfloat16), "dp", scatter_dimension=0, tiled=True
        ).astype(jnp.float32),
        lax.psum_scatter(
            summed[10].astype(jnp.bfloat16), "dp", scatter_dimension=0, tiled=True
        ).astype(jnp.float32),
        lax.psum_scatter(
            summed[11].astype(jnp.bfloat16), "dp", scatter_dimension=0, tiled=True
        ).astype(jnp.float32),
        lax.psum_scatter(
            summed[12].astype(jnp.bfloat16), "dp", scatter_dimension=0, tiled=True
        ).astype(jnp.float32),
        lax.psum_scatter(
            summed[13].astype(jnp.bfloat16), "dp", scatter_dimension=0, tiled=True
        ).astype(jnp.float32),
        lax.psum_scatter(
            summed[14].astype(jnp.bfloat16), "dp", scatter_dimension=0, tiled=True
        ).astype(jnp.float32),
        lax.psum_scatter(
            summed[15].astype(jnp.bfloat16), "dp", scatter_dimension=1, tiled=True
        ).astype(jnp.float32),
        lax.psum_scatter(
            summed[16].astype(jnp.bfloat16), "dp", scatter_dimension=0, tiled=True
        ).astype(jnp.float32),
        lax.psum_scatter(
            summed[17].astype(jnp.bfloat16), "dp", scatter_dimension=1, tiled=True
        ).astype(jnp.float32),
        lax.psum_scatter(
            summed[18].astype(jnp.bfloat16), "dp", scatter_dimension=0, tiled=True
        ).astype(jnp.float32),
        lax.psum_scatter(
            summed[19].astype(jnp.bfloat16), "dp", scatter_dimension=0, tiled=True
        ).astype(jnp.float32),
        lax.psum_scatter(
            summed[20].astype(jnp.bfloat16), "dp", scatter_dimension=0, tiled=True
        ).astype(jnp.float32),
        lax.psum_scatter(tiled.astype(jnp.bfloat16), "dp", scatter_dimension=0, tiled=True).astype(
            jnp.float32
        ),
    )
    return (
        output.astype(jnp.bfloat16).reshape(row_count, span, width),
        grad_hidden,
        shares[0],
        shares[1],
        shares[2],
        shares[3],
        shares[4],
        shares[5],
        shares[6],
        shares[7],
        shares[8],
        shares[21].reshape(shares[21].shape[-1]),
        shares[9],
        shares[10],
        shares[11],
        shares[12],
        shares[13],
        shares[14],
        shares[15],
        shares[16],
        shares[17],
        shares[18],
        shares[19],
        shares[20],
    )


def solution(mesh):
    placed = (
        P("dp", "blk", None),
        P("dp"),
        P("dp", "blk", None),
        P("dp", None),
        P("dp"),
        P("dp", None),
        P("dp", None),
        P("dp"),
        P("dp", None),
        P("dp", None),
        P("dp"),
        P("dp", None),
        P(),
        P("dp", None),
        P("dp"),
        P("dp", None),
        P("dp"),
        P("dp"),
        P("dp"),
        P(None, "dp", None),
        P("dp"),
        P(None, "dp", None),
        P("dp"),
        P("dp"),
        P("dp"),
    )
    return jax.shard_map(
        local,
        mesh=mesh,
        in_specs=placed,
        out_specs=(
            P("dp", "blk", None),
            P("dp", "blk", None),
            P("dp", None),
            P("dp"),
            P("dp", None),
            P("dp", None),
            P("dp"),
            P("dp", None),
            P("dp", None),
            P("dp"),
            P("dp", None),
            P(),
            P("dp", None),
            P("dp"),
            P("dp", None),
            P("dp"),
            P("dp"),
            P("dp"),
            P(None, "dp", None),
            P("dp"),
            P(None, "dp", None),
            P("dp"),
            P("dp"),
            P("dp"),
        ),
        check_vma=False,
    )
```

profile of v0, /device:TPU:0, one launch (start us, length us, event | category | flops | bytes accessed | tf_op | source)
XLA Modules:
  0.0 2064.6 jit_solution(12149564887635217269)
XLA Ops:
  19.2 63.0 %all-reduce.61 = (bf16[384]{0:T(512)(128)(2,1)}, bf16[384]{0:T(512)(128)(2,1)}, bf16[768]{0:T(1024)(128)(2,1)}, bf16[384]{0:T(512)(128)(2,1)}, bf16[384]{0:T(512...) all-reduce(bf16[384]{0:T(512)(128)(2,1)S(1)} %dynamic-update-slice., ...), channel_id=1, replica_groups=mesh['blk'=2,'dp'=16] {'dp'}, use_global_device_ids=true, to_apply=%add.36 | all-reduce | flops 8448 | bytes 33792
  83.1 18.9 all_gather.84
  108.0 21.1 %all_gather.80 = bf16[768,384]{1,0:T(8,128)(2,1)S(1)} all-gather(bf16[48,384]{1,0:T(8,128)(2,1)S(1)} %convert_element_type.445), channel_id=1, replica_groups=mesh['blk'=2,'dp'=16] {'dp'}, dimensions={0}, use_global_device_ids=true | all-gather | bytes 626688 | tf_op jit(solution)/shard_map/all_gather | solution.py:178
  163.1 22.1 %all_gather.88 = bf16[768,384]{1,0:T(8,128)(2,1)} all-gather(bf16[48,384]{1,0:T(8,128)(2,1)S(1)} %convert_element_type.459), channel_id=1, replica_groups=mesh['blk'=2,'dp'=16] {'dp'}, dimensions={0}, use_global_device_ids=true | all-gather | bytes 626688 | tf_op jit(solution)/shard_map/all_gather | solution.py:182
  186.0 20.4 all_gather.82
  208.7 22.1 %all_gather.91 = bf16[768,384]{1,0:T(8,128)(2,1)} all-gather(bf16[48,384]{1,0:T(8,128)(2,1)S(1)} %convert_element_type.465), channel_id=1, replica_groups=mesh['blk'=2,'dp'=16] {'dp'}, dimensions={0}, use_global_device_ids=true | all-gather | bytes 626688 | tf_op jit(solution)/shard_map/all_gather | solution.py:185
  230.8 19.3 all_gather.90
  274.1 18.8 add_convert_fusion.2
  333.2 329.2 %while.34 = (s32[]{:T(128)}, f32[1,6,2048]{2,1,0:T(8,128)S(1)}, f32[1,6,2048]{2,1,0:T(8,128)S(1)}, f32[1,6,2048,64]{2,3,1,0:T(8,128)}, s32[8]{0:T(128)S(1)}, /*i...) while((s32[]{:T(128)}, f32[1,6,2048]{2,1,0:T(8,128)S(1)}, ...), condition=%wide.region_3.4_spmd.clone, body=%wide.region_0.3_spmd.clone.sunk | while | flops 1695888384 | bytes 90707104 | solution.py:118
  675.1 65.4 %fusion.47 = (bf16[2048,2,1536]{2,0,1:T(8,128)(2,1)}, f32[2048,2,1536]{2,0,1:T(8,128)}, f32[2,2048,1536]{2,1,0:T(8,128)}) fusion(f32[2,1536]{1,0:T(2,128)S(1)} %copy-done.93, bf16[2048,2,384]{0,2,1:T(8,128)(2,1)S(1)} %bitcast.572, bf16[2,384,1536]{2,1,0:T(8,128)(2,1)} %all-gather.11.cloned.1.call-done), kind=kOutput, calls=%fused_computation.68 | convolution fusion | flops 5247074304 | bytes 68431872 | tf_op jit(solution)/shard_map/ngi,gio->ngo/dot_general | solution.py:67
  761.2 27.1 %fusion.216 = (bf16[2,1536]{1,0:T(2,128)(2,1)}, bf16[2048,2,1536]{2,0,1:T(8,128)(2,1)}) fusion(f32[2048,2,1536]{2,0,1:T(8,128)} %get-tuple-element.681, bf16[2048,2,384]{0,2,1:T(8,128)(2,1)S(1)} %bitcast.570, bf16[2,1536,384]{2,1,0:T(8,128)(2,1)} %all-gather.13.cloned.1.call-done, f32[2,2048,1536]{2,1,0:T(8,128)} %get-tuple-element.741, ...), kind=kOutput, calls=%fused_computation.312 | convolution fusion | flops 4932498432 | bytes 68438016 | tf_op jit(solution)/shard_map/ngo,gio->ngi/dot_general | solution.py:76
  859.7 577.0 %while.35 = (s32[]{:T(128)}, f32[1,2048,6,64]{1,3,2,0:T(8,128)}, bf16[1,4096,384]{1,2,0:T(8,128)(2,1)}, bf16[1,4096,384]{1,2,0:T(8,128)(2,1)}, bf16[8,1,512,384]...) while((s32[]{:T(128)}, f32[1,2048,6,64]{1,3,2,0:T(8,128)}, ...), condition=%wide.region_16.17_spmd.clone, body=%wide.region_15.16_spmd.clone.sunk | while | flops 4105835520 | bytes 134239472 | solution.py:118
  874.4 17.3 fusion.298
  946.5 17.4 fusion.298
  1436.9 27.4 %convert_multiply_fusion.17 = (f32[1,2048,6,64]{1,3,2,0:T(8,128)}, f32[1,2048,6,64]{1,3,2,0:T(8,128)}, f32[1,2048,6,64]{1,3,2,0:T(8,128)}, f32[1,2048,6,64]{1,3,...) fusion(bf16[1,2048,6,64]{1,3,2,0:T(8,128)(2,1)} %bitcast.565, ...), kind=kLoop, calls=%fused_computation.100 | loop fusion | flops 21909504 | bytes 59080704 | tf_op jit(solution)/shard_map/transpose(jvp())/mul | solution.py:100
  1472.4 32.4 %fusion.73 = (f32[768]{0:T(1024)S(1)}, f32[768]{0:T(1024)S(1)}, f32[768]{0:T(1024)S(1)}, f32[768]{0:T(1024)S(1)}, f32[768]{0:T(1024)S(1)}, /*index=5*/f32[768]{0...) fusion(f32[1,2056,768]{1,2,0:T(8,128)} %copy-done.1, ...), kind=kOutput, calls=%fused_computation.128 | convolution fusion | flops 1242555648 | bytes 63532032 | tf_op jit(solution)/shard_map/dot_general | solution.py:55
  1539.2 25.8 %fusion.201 = (bf16[1,2056,768]{1,2,0:T(8,128)(2,1)}, f32[1,2056,768]{1,2,0:T(8,128)}) fusion(f32[1,2048,768]{1,2,0:T(8,128)} %get-tuple-element.698, f32[1,2048,768]{1,2,0:T(8,128)} %get-tuple-element.697, f32[1,2048,768]{1,2,0:T(8,128)} %get-tuple-element.696, f32[1,2048,768]{1,2,0:T(8,128)} %get-tuple-element.695, ...), kind=kLoop, calls=%fused_computation.300 | loop fusion | flops 14211072 | bytes 66097152 | tf_op jit(solution)/shard_map/convert.19
  1658.8 26.4 %reduce-scatter.37.cloned.1.call-done = bf16[48,384]{1,0:T(8,128)(2,1)} async-done(((bf16[768,384]{1,0:T(8,128)(2,1)}), bf16[48,384]{1,0:T(8,128)(2,1)}) %reduce-scatter.37.cloned.1.call-update) | async-done | bytes 36880
  1686.7 56.3 %reduce-scatter.45.cloned.1.call-done = bf16[48,384]{1,0:T(8,128)(2,1)} async-done(((bf16[768,384]{1,0:T(8,128)(2,1)}), bf16[48,384]{1,0:T(8,128)(2,1)}) %reduce-scatter.45.cloned.1.call-update) | async-done | bytes 36880
  1744.5 26.0 %all-reduce.69.cloned.1.call-done = (bf16[48,768]{1,0:T(8,128)(2,1)}, bf16[2,24,1536]{2,1,0:T(8,128)(2,1)}, bf16[2,96,384]{2,1,0:T(8,128)(2,1)}) async-done(((bf16[48,768]{1,0:T(8,128)(2,1)}, bf16[2,24,1536]{2,1,0:T(8,128)(2,1)}, bf16[2,96,384]{2,1,0:T(8,128)(2,1)}), (bf16[48,768]{1,0:T(8,128)(2,1)}, bf16[2,24,1536]{2,1,0:T(8,128)(2,1)}, bf16[2,96,384]{2,1,0:T(8,128)(2,1)})) %all-reduce.69.cloned.1.call-update) | async-done | bytes 368656 | tf_op jit(solution)/shard_map/psum | solution.py:504
  1777.7 61.5 %all-reduce.60 = (bf16[768]{0:T(1024)(128)(2,1)S(1)}, bf16[384]{0:T(512)(128)(2,1)S(1)}, bf16[384]{0:T(512)(128)(2,1)S(1)}, bf16[384]{0:T(512)(128)(2,1)S(1)}, b...) all-reduce(bf16[768]{0:T(1024)(128)(2,1)} %copy-done.99, ...), channel_id=1, replica_groups=mesh['blk'=2,'dp'=16] {'dp'}, use_global_device_ids=true, to_apply=%add.46 | all-reduce | flops 10848 | bytes 43392
  1888.1 54.2 %reduce-scatter.49.cloned.1.call-done = bf16[24,54]{1,0:T(8,128)(2,1)} async-done(((bf16[384,54]{1,0:T(8,128)(2,1)}), bf16[24,54]{1,0:T(8,128)(2,1)}) %reduce-scatter.49.cloned.1.call-update) | async-done | bytes 2608
  1942.3 58.3 %reduce-scatter.31.cloned.1.call-done = bf16[48,384]{1,0:T(8,128)(2,1)} async-done(((bf16[768,384]{1,0:T(8,128)(2,1)}), bf16[48,384]{1,0:T(8,128)(2,1)}) %reduce-scatter.31.cloned.1.call-update) | async-done | bytes 36880 | tf_op jit(solution)/shard_map/reduce_scatter | solution.py:536
  2013.0 21.8 %all-reduce.67.cloned.1.call-done = (bf16[48,384]{0,1:T(8,128)(2,1)}, bf16[48,384]{0,1:T(8,128)(2,1)}, bf16[48,384]{0,1:T(8,128)(2,1)}, bf16[48,384]{0,1:T(8,128...) async-done(((bf16[48,384]{0,1:T(8,128)(2,1)}, ...) | async-done | bytes 188944 | tf_op jit(solution)/shard_map/psum | solution.py:493
  (693 shorter events, 1304.4 us)
Async XLA Ops:
  7.2 316.5 %all-gather.17.cloned.1.call-start = ((), (), s32[]{:S(2)}) async-start(), calls=%async_computation.18 | async-start | bytes 4718592 | tf_op jit(solution)/shard_map/all_gather | solution.py:295
  107.9 220.6 %all-gather.15.cloned.1.call-start = ((), (), s32[]{:S(2)}) async-start(), calls=%async_computation.17 | async-start | bytes 4718592 | tf_op jit(solution)/shard_map/all_gather | solution.py:294
  132.9 531.8 %all-gather.9.cloned.1.call-start = ((), (), s32[]{:S(2)}) async-start(), calls=%async_computation.12 | async-start | bytes 1253376 | tf_op jit(solution)/shard_map/all_gather | solution.py:187
  134.7 540.4 %all-gather.11.cloned.1.call-start = ((), (), s32[]{:S(2)}) async-start(), calls=%async_computation.13 | async-start | bytes 2506752 | tf_op jit(solution)/shard_map/all_gather | solution.py:191
  135.4 605.0 %all-gather.13.cloned.1.call-start = ((), (), s32[]{:S(2)}) async-start(), calls=%async_computation.14 | async-start | bytes 2506752 | tf_op jit(solution)/shard_map/all_gather | solution.py:193
  137.1 130.2 %collective-permute-start = (bf16[1,4,768]{1,2,0:T(8,128)(2,1)}, bf16[1,4,768]{1,2,0:T(8,128)(2,1)}, u32[]{:S(2)}, u32[]{:S(2)}) collective-permute-start(bf16[1,4,768]{1,2,0:T(8,128)(2,1)} %copy.217), channel_id=1, source_target_pairs={{0,16},{1,17},{2,18},{3,19},{4,20},{5,21},{6,22},{7,23},{8,24},{9,... | collective-permute-start | bytes 18440 | tf_op jit(solution)/shard_map/ppermute | solution.py:27
  142.0 125.3 %collective-permute-start.1 = (bf16[1,4,768]{1,2,0:T(8,128)(2,1)}, bf16[1,4,768]{1,2,0:T(8,128)(2,1)}, u32[]{:S(2)}, u32[]{:S(2)}) collective-permute-start(bf16[1,4,768]{1,2,0:T(8,128)(2,1)} %copy.218), channel_id=1, source_target_pairs={{16,0},{17,1},{18,2},{19,3},{20,4},{21,5},{22,6},{23,7},{24,8},{25... | collective-permute-start | bytes 18440 | tf_op jit(solution)/shard_map/ppermute | solution.py:29
  144.9 1455.6 %reduce-scatter.47.cloned.1.call-start = ((), (), s32[]{:S(2)}) async-start(), calls=%async_computation.27 | async-start | bytes 2506752
  803.3 798.9 %reduce-scatter.33.cloned.1.call-start = ((), (), s32[]{:S(2)}) async-start(), calls=%async_computation.20 | async-start | bytes 1253376 | tf_op jit(solution)/shard_map/reduce_scatter | solution.py:551
  833.4 768.9 %reduce-scatter.35.cloned.1.call-start = ((), (), s32[]{:S(2)}) async-start(), calls=%async_computation.21 | async-start | bytes 2506752 | tf_op jit(solution)/shard_map/reduce_scatter | solution.py:569
  855.6 746.7 %reduce-scatter.27.cloned.1.call-start = ((), (), s32[]{:S(2)}) async-start(), calls=%async_computation.15 | async-start | bytes 4718592 | tf_op jit(solution)/shard_map/reduce_scatter | solution.py:451
  859.7 577.1 %copy-start.43 = (f32[1,2048,6,1]{1,2,3,0:T(8,128)S(1)}, f32[1,2048,6,1]{1,2,3,0:T(8,128)}, u32[]{:S(2)}) copy-start(f32[1,2048,6,1]{1,2,3,0:T(8,128)} %copy-done.42) | copy-start | bytes 147460
  1436.8 172.6 %reduce-scatter.29.cloned.1.call-start = ((), (), s32[]{:S(2)}) async-start(), calls=%async_computation.16 | async-start | bytes 4718592 | tf_op jit(solution)/shard_map/reduce_scatter | solution.py:454
  1472.4 185.0 %reduce-scatter.43.cloned.1.call-start = ((), (), s32[]{:S(2)}) async-start(), calls=%async_computation.25 | async-start | bytes 208896
  1567.8 21.7 %collective-permute-start.3 = (bf16[1,4,1152]{1,2,0:T(8,128)(2,1)}, bf16[1,4,1152]{1,2,0:T(8,128)(2,1)}, u32[]{:S(2)}, u32[]{:S(2)}) collective-permute-start(bf16[1,4,1152]{1,2,0:T(8,128)(2,1)} %pad_maximum_fusion.6), channel_id=1, source_target_pairs={{16,0},{17,1},{18,2},{19,3},{20,4},{21,5},{22,6},{23,7},{24,8},{25... | collective-permute-start | bytes 27656 | tf_op jit(solution)/shard_map/ppermute | solution.py:29
  1569.9 15.9 collective-permute-start.2
  1576.8 108.4 %reduce-scatter.37.cloned.1.call-start = ((), (), s32[]{:S(2)}) async-start(), calls=%async_computation.22 | async-start | bytes 626688
  1585.7 157.2 %reduce-scatter.45.cloned.1.call-start = ((), (), s32[]{:S(2)}) async-start(), calls=%async_computation.26 | async-start | bytes 626688
  1600.5 170.1 %all-reduce.69.cloned.1.call-start = ((), (), s32[]{:S(2)}) async-start(), calls=%async_computation.30 | async-start | bytes 737280 | tf_op jit(solution)/shard_map/psum | solution.py:504
  1602.3 265.7 %reduce-scatter.39.cloned.1.call-start = ((), (), s32[]{:S(2)}) async-start(), calls=%async_computation.23 | async-start | bytes 626688
  1609.1 277.5 %reduce-scatter.41.cloned.1.call-start = ((), (), s32[]{:S(2)}) async-start(), calls=%async_computation.24 | async-start | bytes 626688
  1616.1 326.2 %reduce-scatter.49.cloned.1.call-start = ((), (), s32[]{:S(2)}) async-start(), calls=%async_computation.28 | async-start | bytes 104448
  1629.0 371.7 %reduce-scatter.31.cloned.1.call-start = ((), (), s32[]{:S(2)}) async-start(), calls=%async_computation.19 | async-start | bytes 626688 | tf_op jit(solution)/shard_map/reduce_scatter | solution.py:536
  1647.5 387.4 %all-reduce.67.cloned.1.call-start = ((), (), s32[]{:S(2)}) async-start(), calls=%async_computation.29 | async-start | bytes 891904 | tf_op jit(solution)/shard_map/psum | solution.py:493
  (109 other events, 3846.7 us)
Sparse Core Ops, SparseCore 0:
  108.0 48.2 all-gather.16
  157.8 44.9 all-gather.14
  205.6 38.6 all-gather.8
  247.0 41.1 all-gather.10
  290.4 41.0 all-gather.12
  803.4 63.2 reduce-scatter.46
  870.7 57.1 reduce-scatter.32
  932.2 61.9 reduce-scatter.34
  1436.9 43.6 reduce-scatter.26
  1482.7 43.3 reduce-scatter.28
  1576.9 50.8 reduce-scatter.42
  1631.2 53.8 reduce-scatter.36
  1689.1 53.8 reduce-scatter.44
  1745.9 24.6 all-reduce.68
  1773.9 54.9 reduce-scatter.38
  1832.8 53.7 reduce-scatter.40
  1889.9 52.3 reduce-scatter.48
  1946.7 53.8 reduce-scatter.30
  2005.7 29.1 all-reduce.66
where the time goes:
time: 2080 us; the launch traced here: 2060 us
  matrix products  916 us (44%)
  other arithmetic  344 us (17%)
  blocking collectives  271 us (13%)
  waiting for transfers between devices  261 us (13%)
  local copies, waits for them, and re-layouts  221 us (11%)
    dot_general x16, matrix products, scored(): jnp.einsum('rqhd,rkhd->rhqk', query_heads, key_heads, preferred_element_t...  165 us
    unnamed x26, waiting for transfers between devices  154 us
    dot_general x8, matrix products, backward_step(): jnp.einsum('rqhd,rkhd->rhqk', grad_view, value_heads, preferred_element_t...  137 us
    unnamed x2, blocking collectives  124 us
    dot_general x8, matrix products, forward_step(): jnp.einsum('rhqk,rkhd->rhqd', weights_now.astype(jnp.bfloat16), value_hea...  116 us
    dot_general x8, matrix products, backward_step(): jnp.einsum('rhqk,rqhd->rkhd', probs.astype(jnp.bfloat16), grad_view, pref...  94.4 us
    reduce_sum x8, other arithmetic, forward_step(): total = total * factor + jnp.sum(weights_now, axis=-1)  93.2 us
    unnamed x283, local copies, waits for them, and re-layouts  79.5 us
  transfers between devices with their start and end apart: 23, of which 7 were waited for; matrix products, arithmetic and copies ran while one was open for 66% of the time, Pallas kernels for 0%

commit v1 on v0

v1 whole, which is shorter than its diff:
```python
import functools, math
import jax, jax.numpy as jnp
from jax import lax
from jax.experimental import pallas as pl
from jax.experimental.pallas import tpu as pltpu
from jax.sharding import PartitionSpec as P

HEADS = 6
HD = 64
KSIZE = 9
REACH = 4
ATT = 384
EPS = 1e-12
BF = jnp.bfloat16
F32 = jnp.float32
MIB = 2**20
EXCLUDED = 2.0**100
SAFE_SCORE = 50.0


def mm(left, right):
    return jnp.dot(left, right, preferred_element_type=F32)


def mm_nt(left, right):
    return lax.dot_general(left, right, (((1,), (1,)), ((), ())), preferred_element_type=F32)


def mm_tn(left, right):
    return lax.dot_general(left, right, (((0,), (0,)), ((), ())), preferred_element_type=F32)


def in_lanes(rows, columns):
    lane = lax.broadcasted_iota(jnp.int32, (rows, 128), 1)
    out = jnp.zeros((rows, 128), F32)
    for at, column in enumerate(columns):
        out = jnp.where(lane == at, column, out)
    return out.astype(BF)


def in_rows(columns, rows):
    row = lax.broadcasted_iota(jnp.int32, (16, columns), 0)
    out = jnp.zeros((16, columns), F32)
    for at, values in enumerate(rows):
        out = jnp.where(row == at, values, out)
    return out.astype(BF)


def three_parts(values):
    high = values.astype(BF).astype(F32)
    rest = values - high
    middle = rest.astype(BF).astype(F32)
    return high, middle, (rest - middle).astype(BF).astype(F32)


def put_head(ref, head, values):
    odd = lax.rem(head, 2) == 1
    none = jnp.zeros_like(values)
    ref[0:HD, :] = jnp.where(odd, none, values)
    ref[HD : 2 * HD, :] = jnp.where(odd, values, none)


def attend_kernel(keys, queries, chunk, at_ref, q_ref, k_ref, v_ref, norm_ref, o_ref, p_ref, key_side, query_side):
    head, tile = pl.program_id(0), pl.program_id(1)
    separator, first_query, first_key = at_ref[0], at_ref[1], at_ref[2]

    @pl.when((head == 0) & (tile == 0))
    def start():
        position = first_key + lax.broadcasted_iota(jnp.int32, (keys, 128), 0)
        late = (position >= separator).astype(F32)
        key_side[...] = in_lanes(keys, [1.0 - late, late, 1.0, 1.0, 1.0])
        query_side[2 * HD + 16 :, :] = jnp.zeros((2 * HD - 16, queries), BF)

    put_head(query_side, head, q_ref[...])
    position = first_query + tile * queries + lax.broadcasted_iota(jnp.int32, (16, queries), 1)
    late = (position >= separator).astype(F32)
    excluded = [-EXCLUDED * late, -EXCLUDED * (1.0 - late)]
    query_side[2 * HD : 2 * HD + 16, :] = in_rows(queries, excluded)
    o_ref[0, HD + 8 : HD + 16, :] = jnp.zeros((8, queries), F32)
    wide = q_ref[...].astype(F32)
    largest = jnp.max(jnp.sum(wide * wide, axis=0, keepdims=True)) * jnp.max(norm_ref[...])

    def scores(at):
        part = slice(at * chunk, (at + 1) * chunk)
        return mm(
            jnp.concatenate([k_ref[part, :], key_side[part, :]], axis=1), query_side[...]
        )

    @pl.when(jnp.logical_not(largest <= SAFE_SCORE * SAFE_SCORE))
    def shifted():
        best = jnp.full((1, queries), -4.0 * EXCLUDED, F32)
        for at in range(keys // chunk):
            best = jnp.maximum(best, jnp.max(scores(at), axis=0, keepdims=True))
        parts = three_parts(jnp.where(best < -0.5 * EXCLUDED, 0.0, best))
        query_side[2 * HD : 2 * HD + 16, :] = in_rows(queries, excluded + [-part for part in parts])
        o_ref[0, HD + 8 : HD + 16, :] = jnp.broadcast_to(
            jnp.where(best < -0.5 * EXCLUDED, best, parts[0] + parts[1] + parts[2]), (8, queries)
        )

    ones = in_rows(chunk, [1.0])
    total = jnp.zeros((HD + 16, queries), F32)
    for at in range(keys // chunk):
        part = slice(at * chunk, (at + 1) * chunk)
        probs = jnp.exp(scores(at)).astype(BF)
        p_ref[0, part, :] = probs
        total = total + mm(jnp.concatenate([v_ref[:, part], ones], axis=0), probs)
    o_ref[0, 0 : HD + 8, :] = total[0 : HD + 8, :]


def attend(at, query_t, key, value_t, norms):
    tokens, keys = query_t.shape[1], key.shape[0]
    queries, chunk = math.gcd(tokens, 1024), math.gcd(keys, 512)
    return pl.pallas_call(
        functools.partial(attend_kernel, keys, queries, chunk),
        grid=(HEADS, tokens // queries),
        in_specs=[
            pl.BlockSpec(memory_space=pltpu.SMEM),
            pl.BlockSpec((HD, queries), lambda h, i: (h, i)),
            pl.BlockSpec((keys, 2 * HD), lambda h, i: (0, h // 2)),
            pl.BlockSpec((HD, keys), lambda h, i: (h, 0)),
            pl.BlockSpec(norms.shape, lambda h, i: (0, 0)),
        ],
        out_specs=[
            pl.BlockSpec((1, HD + 16, queries), lambda h, i: (h, 0, i)),
            pl.BlockSpec((1, keys, queries), lambda h, i: (h, 0, i)),
        ],
        out_shape=[
            jax.ShapeDtypeStruct((HEADS, HD + 16, tokens), F32),
            jax.ShapeDtypeStruct((HEADS, keys, tokens), BF),
        ],
        scratch_shapes=[pltpu.VMEM((keys, 128), BF), pltpu.VMEM((4 * HD, queries), BF)],
        compiler_params=pltpu.CompilerParams(vmem_limit_bytes=56 * MIB),
        cost_estimate=pl.CostEstimate(
            flops=16 * ATT * tokens * keys,
            bytes_accessed=2 * HEADS * tokens * keys,
            transcendentals=HEADS * tokens * keys,
        ),
        name="attend",
    )(at, query_t, key, value_t, norms)


def attend_back_kernel(keys, queries, chunk, p_ref, v_ref, kt_ref, g_ref, side_ref, q_ref, dq_ref, dk_ref, dv_ref, value_side, grad_side, dk_sum, dv_sum):
    head, tile = pl.program_id(0), pl.program_id(1)

    @pl.when((head == 0) & (tile == 0))
    def start():
        value_side[...] = in_lanes(chunk, [1.0, 1.0, 1.0])
        grad_side[2 * HD + 16 :, :] = jnp.zeros((2 * HD - 16, queries), BF)

    @pl.when(tile == 0)
    def fresh():
        dk_sum[...] = jnp.zeros_like(dk_sum)
        dv_sum[...] = jnp.zeros_like(dv_sum)

    put_head(grad_side, head, g_ref[...])
    grad_side[2 * HD : 2 * HD + 16, :] = side_ref[0]
    total = jnp.zeros((HD, queries), F32)
    for at in range(keys // chunk):
        part = slice(at * chunk, (at + 1) * chunk)
        probs = p_ref[0, part, :]
        spread = mm(jnp.concatenate([v_ref[part, :], value_side[...]], axis=1), grad_side[...])
        grad_scores = (probs.astype(F32) * spread).astype(BF)
        dv_sum[:, part] += mm_nt(g_ref[...], probs)
        dk_sum[:, part] += mm_nt(q_ref[...], grad_scores)
        total = total + mm(kt_ref[:, part], grad_scores)
    dq_ref[...] = total * (HD**-0.5)

    @pl.when(tile == pl.num_programs(1) - 1)
    def finish():
        dk_ref[...] = dk_sum[...].astype(dk_ref.dtype)
        dv_ref[...] = dv_sum[...].astype(dv_ref.dtype)


def attend_back(probs, value, key_t, grad_t, side, query_t, out_type):
    tokens, keys = query_t.shape[1], value.shape[0]
    queries, chunk = math.gcd(tokens, 512), math.gcd(keys, 512)
    by_token = pl.BlockSpec((HD, queries), lambda h, i: (h, i))
    by_key = pl.BlockSpec((HD, keys), lambda h, i: (h, 0))
    return pl.pallas_call(
        functools.partial(attend_back_kernel, keys, queries, chunk),
        grid=(HEADS, tokens // queries),
        in_specs=[
            pl.BlockSpec((1, keys, queries), lambda h, i: (h, 0, i)),
            pl.BlockSpec((keys, 2 * HD), lambda h, i: (0, h // 2)),
            by_key,
            by_token,
            pl.BlockSpec((1, 16, queries), lambda h, i: (h, 0, i)),
            by_token,
        ],
        out_specs=[by_token, by_key, by_key],
        out_shape=[
            jax.ShapeDtypeStruct((ATT, tokens), F32),
            jax.ShapeDtypeStruct((ATT, keys), out_type),
            jax.ShapeDtypeStruct((ATT, keys), out_type),
        ],
        scratch_shapes=[
            pltpu.VMEM((chunk, 128), BF),
            pltpu.VMEM((4 * HD, queries), BF),
            pltpu.VMEM((HD, keys), F32),
            pltpu.VMEM((HD, keys), F32),
        ],
        compiler_params=pltpu.CompilerParams(vmem_limit_bytes=56 * MIB),
        cost_estimate=pl.CostEstimate(
            flops=32 * ATT * tokens * keys,
            bytes_accessed=2 * HEADS * tokens * keys,
            transcendentals=0,
        ),
        name="attend_back",
    )(probs, value, key_t, grad_t, side, query_t)


def all_of(shape):
    return pl.BlockSpec(shape, lambda *at: (0,) * len(shape))


def rows_of(rows, width):
    return pl.BlockSpec((rows, width), lambda i: (i, 0))


def columns_of(height, columns):
    return pl.BlockSpec((height, columns), lambda i: (0, i))


def run_tiles(kernel, name, steps, inputs, outputs, scratch, flops):
    args, in_specs = zip(*inputs)
    shapes, out_specs = zip(*outputs)
    size = sum(math.prod(v.shape) * v.dtype.itemsize for v in args + shapes)
    return pl.pallas_call(
        kernel,
        grid=(steps,),
        in_specs=list(in_specs),
        out_specs=list(out_specs),
        out_shape=list(shapes),
        scratch_shapes=scratch,
        compiler_params=pltpu.CompilerParams(vmem_limit_bytes=60 * MIB),
        cost_estimate=pl.CostEstimate(flops=flops, bytes_accessed=size, transcendentals=0),
        name=name,
    )(*args)


def shaped(shape, dtype):
    return jax.ShapeDtypeStruct(shape, dtype)


def project_kernel(parts, x_ref, w_ref, bias_ref, bias_t_ref, *refs):
    norm_ref, flipped = refs[2 * parts], refs[2 * parts + 1]

    @pl.when(pl.program_id(0) == 0)
    def start():
        norm_ref[...] = jnp.zeros_like(norm_ref)
        flipped[...] = w_ref[...].T

    x = x_ref[...]
    plain = mm(x, w_ref[...]) + bias_ref[...]
    turned = mm_nt(flipped[...], x) + bias_t_ref[...]
    for part in range(parts):
        own = slice(part * ATT, (part + 1) * ATT)
        refs[2 * part][...] = plain[:, own].astype(BF)
        across = turned[own].astype(BF)
        if part == parts - 2:
            wide = across.astype(F32)
            for head in range(HEADS):
                cells = wide[head * HD : (head + 1) * HD]
                size = jnp.sum(cells * cells, axis=0, keepdims=True)
                norm_ref[...] = jnp.maximum(norm_ref[...], size)
        if part < parts - 2:
            across = (turned[own].astype(BF).astype(F32) * (HD**-0.5)).astype(BF)
        refs[2 * part + 1][...] = across


def project(x, weight, bias):
    tokens, width = x.shape
    parts = weight.shape[1] // ATT
    tile = math.gcd(tokens, 512)
    outputs = []
    for part in range(parts):
        outputs.append((shaped((tokens, ATT), BF), rows_of(tile, ATT)))
        outputs.append((shaped((ATT, tokens), BF), columns_of(ATT, tile)))
    outputs.append((shaped((8, tile), F32), all_of((8, tile))))
    return run_tiles(
        functools.partial(project_kernel, parts),
        "project",
        tokens // tile,
        [
            (x, rows_of(tile, width)),
            (weight, all_of(weight.shape)),
            (bias, all_of(bias.shape)),
            (bias.reshape(-1, 1), all_of((bias.shape[1], 1))),
        ],
        outputs,
        [pltpu.VMEM((weight.shape[1], width), BF)],
        4 * tokens * width * weight.shape[1],
    )


def fill_window(window, x_ref, halo_ref, tile, rows):
    first = tile * rows
    tokens = x_ref.shape[0]
    before = x_ref[pl.ds(pl.multiple_of(jnp.maximum(first - 16, 0), 16), 16), :]
    after = x_ref[pl.ds(pl.multiple_of(jnp.minimum(first + rows, tokens - 16), 16), 16), :]
    window[0:16, :] = jnp.where(tile == 0, halo_ref[0:16, :], before).astype(window.dtype)
    window[16 : 16 + rows, :] = x_ref[pl.ds(pl.multiple_of(first, rows), rows), :].astype(window.dtype)
    window[16 + rows :, :] = jnp.where(
        tile == pl.num_programs(0) - 1, halo_ref[16:32, :], after
    ).astype(window.dtype)


def fill_spread(spread):
    row = lax.broadcasted_iota(jnp.int32, (128, ATT), 0)
    head = lax.broadcasted_iota(jnp.int32, (128, ATT), 1) // HD
    for tap in range(KSIZE):
        spread[:, tap * ATT : (tap + 1) * ATT] = (row == tap * 8 + head).astype(F32).astype(BF)


def mix_kernel(rows, at_ref, x_ref, halo_ref, q_ref, taps_ref, wc_ref, bc_ref, wp_ref, bp_ref, wk_ref, bk_ref, depth_ref, keyconv_ref, attn_ref, kernt_ref, kern_ref, conv_ref, out_ref, rim_ref, window, conv_window, spread):
    tile = pl.program_id(0)
    last = pl.num_programs(0) - 1

    @pl.when(tile == 0)
    def start():
        fill_spread(spread)

    fill_window(window, x_ref, halo_ref, tile, rows)
    width = window.shape[1]
    for at in range(0, width, 128):
        some = slice(at, at + 128)
        total = jnp.zeros((rows, 128), F32)
        for tap in range(KSIZE):
            total = total + window[12 + tap : 12 + tap + rows, some] * taps_ref[tap : tap + 1, some]
        depth_ref[:, some] = total.astype(BF)
    position = (
        at_ref[1] + tile * rows - 16 + lax.broadcasted_iota(jnp.int32, (rows + 32, ATT), 0)
    )
    inside = (position >= 0) & (position < at_ref[3])
    values = mm(window[...].astype(BF), wc_ref[...]) + bc_ref[...]
    values = jnp.where(inside, values, 0.0).astype(BF)
    out_ref[...] = values[16 : 16 + rows]

    @pl.when(tile == 0)
    def first_rim():
        rim_ref[0:16, :] = values[0:16]

    @pl.when(tile == last)
    def last_rim():
        rim_ref[16:32, :] = values[16 + rows :]

    conv_window[...] = values.astype(F32)
    keyconv = mm(depth_ref[...], wp_ref[...]) + bp_ref[...]
    keyconv_ref[...] = keyconv
    attn_key = (keyconv * q_ref[...].astype(F32)).astype(BF)
    attn_ref[...] = attn_key
    logits = mm_nt(wk_ref[...], attn_key) + bk_ref[...]
    slabs = [logits[8 * tap : 8 * tap + 8] for tap in range(KSIZE)]
    best = functools.reduce(jnp.maximum, slabs)
    slabs = [jnp.exp(slab - best) for slab in slabs]
    share = 1.0 / functools.reduce(jnp.add, slabs)
    slabs = [slab * share for slab in slabs]
    kernt = jnp.concatenate(slabs + [jnp.zeros((128 - 8 * KSIZE, rows), F32)], axis=0)
    kernt_ref[...] = kernt[0 : 8 * KSIZE]
    kern = kernt.astype(BF).T
    kern_ref[...] = kern
    total = jnp.zeros((rows, ATT), F32)
    for tap in range(KSIZE):
        total = total + mm(kern, spread[:, tap * ATT : (tap + 1) * ATT]) * conv_window[12 + tap : 12 + tap + rows, :]
    conv_ref[...] = total.astype(BF)


def mix(at, x, halo, query, taps, w_convout, b_convout, w_point, b_keyconv, w_kernel, kernel_bias):
    tokens, width = x.shape
    rows = math.gcd(tokens, 256)
    whole = [(v, all_of(v.shape)) for v in (taps, w_convout, b_convout, w_point, b_keyconv, w_kernel, kernel_bias)]
    return run_tiles(
        functools.partial(mix_kernel, rows),
        "mix",
        tokens // rows,
        [
            (at, pl.BlockSpec(memory_space=pltpu.SMEM)),
            (x, all_of(x.shape)),
            (halo, all_of(halo.shape)),
            (query, rows_of(rows, ATT)),
        ]
        + whole,
        [
            (shaped((tokens, width), BF), rows_of(rows, width)),
            (shaped((tokens, ATT), F32), rows_of(rows, ATT)),
            (shaped((tokens, ATT), BF), rows_of(rows, ATT)),
            (shaped((8 * KSIZE, tokens), F32), columns_of(8 * KSIZE, rows)),
            (shaped((tokens, 128), BF), rows_of(rows, 128)),
            (shaped((tokens, ATT), BF), rows_of(rows, ATT)),
            (shaped((tokens, ATT), BF), rows_of(rows, ATT)),
            (shaped((32, ATT), BF), all_of((32, ATT))),
        ],
        [
            pltpu.VMEM((rows + 32, width), F32),
            pltpu.VMEM((rows + 32, ATT), F32),
            pltpu.VMEM((128, KSIZE * ATT), BF),
        ],
        4 * tokens * width * ATT * 4,
    )


def normal(values):
    centre = values - jnp.mean(values, axis=-1, keepdims=True)
    scale = lax.rsqrt(jnp.mean(centre * centre, axis=-1, keepdims=True) + EPS)
    return centre * scale, scale


def normal_back(grad, unit, scale):
    return scale * (
        grad
        - jnp.mean(grad, axis=-1, keepdims=True)
        - unit * jnp.mean(grad * unit, axis=-1, keepdims=True)
    )


def gelu_parts(values):
    size = jnp.abs(values)
    t = 1.0 / (1.0 + (0.3275911 * math.sqrt(0.5)) * size)
    tail = t * (
        0.5 * 0.254829592
        + t * (0.5 * -0.284496736 + t * (0.5 * 1.421413741 + t * (0.5 * -1.453152027 + t * (0.5 * 1.061405429))))
    )
    bell = jnp.exp(-0.5 * values * values)
    tail = tail * bell
    share = jnp.where(values < 0.0, tail, 1.0 - tail)
    return values * share, share + values * (bell * (1.0 / math.sqrt(2.0 * math.pi)))


def middle_kernel(blocks, rows, units, *refs):
    o_refs, refs = refs[:blocks], refs[blocks:]
    (conv_ref, x_ref, og_ref, wd_ref, wu_ref, wn_ref, vec_ref, bu_ref), refs = refs[:8], refs[8:]
    (out_ref, sum_ref, gconv_ref), refs = refs[:3], refs[3:]
    g_refs, refs = refs[:blocks], refs[blocks:]
    side_refs, refs = refs[:blocks], refs[blocks:]
    (gwd_ref, gwu_ref, gwn_ref, gvec_ref, gbu_ref, wd_sum, wu_sum, wn_sum, acts, slopes) = refs
    tile = pl.program_id(0)
    hidden_units = wu_ref.shape[1]
    groups = 2
    inner = ATT
    outer = hidden_units // groups

    @pl.when(tile == 0)
    def start():
        for ref in (wd_sum, wu_sum, wn_sum, gvec_ref, gbu_ref):
            ref[...] = jnp.zeros_like(ref)

    shifts = [ref[:, HD + 8 : HD + 9, :] for ref in o_refs]
    top = functools.reduce(jnp.maximum, shifts)
    weights = [jnp.exp(shift - top) for shift in shifts]
    mass = functools.reduce(jnp.add, [w * ref[:, HD : HD + 1, :] for w, ref in zip(weights, o_refs)])
    weights = [w / mass for w in weights]
    heads = functools.reduce(jnp.add, [w * ref[:, 0:HD, :] for w, ref in zip(weights, o_refs)])
    att_t = heads.reshape(ATT, rows).astype(BF)
    conv = conv_ref[...]
    vec = [vec_ref[at : at + 1, :] for at in range(6)]
    dense = mm(att_t.T, wd_ref[0:ATT, :]) + mm(conv, wd_ref[ATT:, :]) + vec[0]
    unit_one, scale_one = normal(dense + x_ref[...].astype(F32))
    normed = unit_one * vec[1] + vec[2]
    low = normed.astype(BF)
    downs = []
    for group in range(groups):
        mine = low[:, group * inner : (group + 1) * inner]
        down = jnp.zeros((rows, inner), F32)
        for at in range(0, outer, units):
            here = slice(group * outer + at, group * outer + at + units)
            upward = mm(mine, wu_ref[:, here]) + bu_ref[:, here]
            act, slope = gelu_parts(upward)
            act = act.astype(BF)
            acts[:, here] = act
            slopes[:, here] = slope.astype(BF)
            down = down + mm(act, wn_ref[at : at + units, group * inner : (group + 1) * inner])
        downs.append(down)
    unit_two, scale_two = normal(jnp.concatenate(downs, axis=1) + vec[3] + normed)
    out_ref[...] = (unit_two * vec[4] + vec[5]).astype(BF)
    og = og_ref[...].astype(F32)
    gvec_ref[4:5, :] += jnp.sum(og * unit_two, axis=0, keepdims=True)
    gvec_ref[5:6, :] += jnp.sum(og, axis=0, keepdims=True)
    grad_two = normal_back(og * vec[4], unit_two, scale_two)
    grad_down = grad_two.astype(BF)
    gvec_ref[3:4, :] += jnp.sum(grad_down.astype(F32), axis=0, keepdims=True)
    backs = []
    for group in range(groups):
        lanes = slice(group * inner, (group + 1) * inner)
        mine, grads = low[:, lanes], grad_down[:, lanes]
        mine_t = mine.T
        back = jnp.zeros((rows, inner), F32)
        for at in range(0, outer, units):
            here = slice(group * outer + at, group * outer + at + units)
            grad_act = mm_nt(grads, wn_ref[at : at + units, lanes])
            grad_up = (grad_act * slopes[:, here].astype(F32)).astype(BF)
            gbu_ref[0:1, here] += jnp.sum(grad_up.astype(F32), axis=0, keepdims=True)
            wn_sum[at : at + units, lanes] += mm_tn(acts[:, here], grads)
            wu_sum[:, here] += mm(mine_t, grad_up)
            back = back + mm_nt(grad_up, wu_ref[:, here])
        backs.append(back)
    grad_normed = grad_two + jnp.concatenate(backs, axis=1)
    gvec_ref[1:2, :] += jnp.sum(grad_normed * unit_one, axis=0, keepdims=True)
    gvec_ref[2:3, :] += jnp.sum(grad_normed, axis=0, keepdims=True)
    grad_one = normal_back(grad_normed * vec[1], unit_one, scale_one)
    sum_ref[...] = grad_one
    grad_dense = grad_one.astype(BF)
    gvec_ref[0:1, :] += jnp.sum(grad_dense.astype(F32), axis=0, keepdims=True)
    wd_sum[0:ATT, :] += mm(att_t, grad_dense)
    wd_sum[ATT:, :] += mm_tn(conv, grad_dense)
    gconv_ref[...] = mm_nt(grad_dense, wd_ref[ATT:, :]).astype(BF)
    grad_att = mm_nt(wd_ref[0:ATT, :], grad_dense).astype(BF).astype(F32).reshape(HEADS, HD, rows)
    for weight, g_ref, side_ref in zip(weights, g_refs, side_refs):
        share = (grad_att * weight).astype(BF)
        g_ref[...] = share.reshape(ATT, rows)
        delta = -jnp.sum(share.astype(F32) * heads, axis=1, keepdims=True)
        row = lax.broadcasted_iota(jnp.int32, (HEADS, 16, rows), 1)
        side = jnp.zeros((HEADS, 16, rows), F32)
        for at, part in enumerate(three_parts(delta)):
            side = jnp.where(row == at, part, side)
        side_ref[...] = side.astype(BF)

    @pl.when(tile == pl.num_programs(0) - 1)
    def finish():
        gwd_ref[...] = wd_sum[...].astype(BF)
        gwu_ref[...] = wu_sum[...].astype(BF)
        gwn_ref[...] = wn_sum[...].astype(BF)


def middle(outs, conv, x, out_grad, w_dense, w_up, w_down, vectors, b_up):
    tokens, width = x.shape
    rows = math.gcd(tokens, 256)
    blocks = len(outs)
    heads = pl.BlockSpec((HEADS, HD + 16, rows), lambda i: (0, 0, i))
    side = pl.BlockSpec((HEADS, 16, rows), lambda i: (0, 0, i))
    once = [(v, all_of(v.shape)) for v in (w_dense, w_up, w_down, vectors, b_up)]
    results = run_tiles(
        functools.partial(middle_kernel, blocks, rows, 512),
        "middle",
        tokens // rows,
        [(o, heads) for o in outs]
        + [
            (conv, rows_of(rows, ATT)),
            (x, rows_of(rows, width)),
            (out_grad, rows_of(rows, width)),
        ]
        + once,
        [
            (shaped((tokens, width), BF), rows_of(rows, width)),
            (shaped((tokens, width), F32), rows_of(rows, width)),
            (shaped((tokens, ATT), BF), rows_of(rows, ATT)),
        ]
        + [(shaped((ATT, tokens), BF), columns_of(ATT, rows))] * blocks
        + [(shaped((HEADS, 16, tokens), BF), side)] * blocks
        + [
            (shaped(w_dense.shape, BF), all_of(w_dense.shape)),
            (shaped(w_up.shape, BF), all_of(w_up.shape)),
            (shaped(w_down.shape, BF), all_of(w_down.shape)),
            (shaped((8, width), F32), all_of((8, width))),
            (shaped((8, w_up.shape[1]), F32), all_of((8, w_up.shape[1]))),
        ],
        [
            pltpu.VMEM(w_dense.shape, F32),
            pltpu.VMEM(w_up.shape, F32),
            pltpu.VMEM(w_down.shape, F32),
            pltpu.VMEM((rows, w_up.shape[1]), BF),
            pltpu.VMEM((rows, w_up.shape[1]), BF),
        ],
        6 * tokens * (w_dense.size + w_up.size + w_down.size),
    )
    output, grad_sum, grad_conv = results[:3]
    return output, grad_sum, grad_conv, results[3 : 3 + blocks], results[3 + blocks : 3 + 2 * blocks], results[3 + 2 * blocks :]


def mix_back_kernel(rows, x_ref, halo_ref, values_ref, rim_ref, gconv_ref, kernt_ref, kern_ref, q_ref, keyconv_ref, attn_ref, depth_ref, wp_ref, wk_ref, gq_ref, gdepth_ref, gvalues_ref, gwp_ref, gwk_ref, gbias_ref, gtaps_ref, window, conv_window, summed, products, spread, wp_sum):
    tile = pl.program_id(0)

    @pl.when(tile == 0)
    def start():
        fill_spread(spread)
        for ref in (gvalues_ref, wp_sum, gwk_ref, gbias_ref, gtaps_ref):
            ref[...] = jnp.zeros_like(ref)

    fill_window(window, x_ref, halo_ref, tile, rows)
    fill_window(conv_window, values_ref, rim_ref, tile, rows)
    summed[...] = jnp.zeros_like(summed)
    grad_conv = gconv_ref[...].astype(F32)
    for tap in range(KSIZE):
        here = slice(tap * ATT, (tap + 1) * ATT)
        there = slice(12 + tap, 12 + tap + rows)
        products[:, here] = (grad_conv * conv_window[there, :]).astype(BF)
        summed[there, :] += mm(kern_ref[...], spread[:, here]) * grad_conv
    first = pl.multiple_of(tile * rows, rows)
    gvalues_ref[pl.ds(first, rows + 32), :] += summed[...]
    grad_kernel = mm_nt(spread[...], products[...])
    slabs = [slice(8 * tap, 8 * tap + 8) for tap in range(KSIZE)]
    kernels = [kernt_ref[slab, :] for slab in slabs]
    mean = functools.reduce(jnp.add, [k * grad_kernel[slab] for k, slab in zip(kernels, slabs)])
    grad_logits = jnp.concatenate(
        [k * (grad_kernel[slab] - mean) for k, slab in zip(kernels, slabs)], axis=0
    ).astype(BF)
    wide_logits = grad_logits.astype(F32)
    gbias_ref[...] += jnp.concatenate(
        [
            jnp.broadcast_to(jnp.sum(wide_logits, axis=1, keepdims=True), (8 * KSIZE, 128)),
            jnp.zeros((8, 128), F32),
        ],
        axis=0,
    )
    gwk_ref[0 : 8 * KSIZE, :] += mm(grad_logits, attn_ref[...])
    grad_attn = mm_tn(grad_logits, wk_ref[...]).astype(BF).astype(F32)
    grad_keyconv = (grad_attn * q_ref[...].astype(F32)).astype(BF)
    gq_ref[...] = grad_attn * keyconv_ref[...]
    gwk_ref[8 * KSIZE : 8 * KSIZE + 1, :] += jnp.sum(grad_keyconv.astype(F32), axis=0, keepdims=True)
    wp_sum[...] += mm_tn(depth_ref[...], grad_keyconv)
    grad_depth = mm_nt(grad_keyconv, wp_ref[...]).astype(BF)
    gdepth_ref[...] = grad_depth
    wide = grad_depth.astype(F32)
    for at in range(0, window.shape[1], 128):
        some = slice(at, at + 128)
        for tap in range(KSIZE):
            gtaps_ref[tap : tap + 1, some] += jnp.sum(
                wide[:, some] * window[12 + tap : 12 + tap + rows, some], axis=0, keepdims=True
            )

    @pl.when(tile == pl.num_programs(0) - 1)
    def finish():
        gwp_ref[...] = wp_sum[...].astype(BF)


def mix_back(x, halo, values, rim, grad_conv, kernt, kern, query, keyconv, attn_key, depth, w_point, w_kernel):
    tokens, width = x.shape
    rows = math.gcd(tokens, 256)
    by_rows = [(v, rows_of(rows, v.shape[1])) for v in (kern, query, keyconv, attn_key, depth)]
    return run_tiles(
        functools.partial(mix_back_kernel, rows),
        "mix_back",
        tokens // rows,
        [(v, all_of(v.shape)) for v in (x, halo, values, rim)]
        + [(grad_conv, rows_of(rows, ATT)), (kernt, columns_of(8 * KSIZE, rows))]
        + by_rows
        + [(v, all_of(v.shape)) for v in (w_point, w_kernel)],
        [
            (shaped((tokens, ATT), F32), rows_of(rows, ATT)),
            (shaped((tokens, width), BF), rows_of(rows, width)),
            (shaped((tokens + 32, ATT), F32), all_of((tokens + 32, ATT))),
            (shaped(w_point.shape, BF), all_of(w_point.shape)),
            (shaped((8 * KSIZE + 8, ATT), F32), all_of((8 * KSIZE + 8, ATT))),
            (shaped((8 * KSIZE + 8, 128), F32), all_of((8 * KSIZE + 8, 128))),
            (shaped((16, width), F32), all_of((16, width))),
        ],
        [
            pltpu.VMEM((rows + 32, width), F32),
            pltpu.VMEM((rows + 32, ATT), F32),
            pltpu.VMEM((rows + 32, ATT), F32),
            pltpu.VMEM((rows, KSIZE * ATT), BF),
            pltpu.VMEM((128, KSIZE * ATT), BF),
            pltpu.VMEM(w_point.shape, F32),
        ],
        4 * tokens * width * ATT * 4,
    )


def finish_kernel(blocks, rows, *refs):
    dq_refs, refs = refs[:blocks], refs[blocks:]
    dk_refs, refs = refs[:blocks], refs[blocks:]
    dv_refs, refs = refs[:blocks], refs[blocks:]
    (x_ref, gq_ref, gvalues_ref, rim_ref, gdepth_ref, halo_ref, sum_ref, w_ref, taps_ref), refs = refs[:9], refs[9:]
    gh_ref, gw_ref, gb_ref, window, w_sum, grads = refs
    tile = pl.program_id(0)
    last = pl.num_programs(0) - 1

    @pl.when(tile == 0)
    def start():
        w_sum[...] = jnp.zeros_like(w_sum)
        gb_ref[...] = jnp.zeros_like(gb_ref)

    def total(some):
        return functools.reduce(jnp.add, [ref[...].astype(F32) for ref in some])

    grads[:, 0:ATT] = (total(dq_refs).T + gq_ref[...]).astype(BF)
    grads[:, ATT : 2 * ATT] = total(dk_refs).astype(BF).T
    grads[:, 2 * ATT : 3 * ATT] = total(dv_refs).astype(BF).T
    first = pl.multiple_of(tile * rows, rows)
    own = gvalues_ref[pl.ds(first + 16, rows), :]
    zero = jnp.zeros((16, ATT), F32)
    before = jnp.where(tile == 0, rim_ref[0:16, :].astype(F32), zero)
    after = jnp.where(tile == last, rim_ref[16:32, :].astype(F32), zero)
    own = jnp.concatenate([own[0:16] + before, own[16 : rows - 16], own[rows - 16 :] + after], axis=0)
    grads[:, 3 * ATT :] = own.astype(BF)
    every = grads[...]
    gb_ref[0:1, :] += jnp.sum(every.astype(F32), axis=0, keepdims=True)
    w_sum[...] += mm(x_ref[...].T, every)
    back = mm_nt(every, w_ref[...])
    fill_window(window, gdepth_ref, halo_ref, tile, rows)
    for at in range(0, window.shape[1], 128):
        some = slice(at, at + 128)
        depth = back[:, some] + sum_ref[:, some]
        for tap in range(KSIZE):
            depth = depth + window[20 - tap : 20 - tap + rows, some] * taps_ref[tap : tap + 1, some]
        gh_ref[:, some] = depth.astype(BF)

    @pl.when(tile == last)
    def finish():
        gw_ref[...] = w_sum[...].astype(BF)


def finish(dqs, dks, dvs, x, grad_query, grad_values, rim, grad_depth, halo, grad_sum, weight, taps):
    tokens, width = x.shape
    rows = math.gcd(tokens, 256)
    blocks = len(dqs)
    return run_tiles(
        functools.partial(finish_kernel, blocks, rows),
        "finish",
        tokens // rows,
        [(v, columns_of(ATT, rows)) for v in list(dqs) + list(dks) + list(dvs)]
        + [
            (x, rows_of(rows, width)),
            (grad_query, rows_of(rows, ATT)),
            (grad_values, all_of(grad_values.shape)),
            (rim, all_of(rim.shape)),
            (grad_depth, all_of(grad_depth.shape)),
            (halo, all_of(halo.shape)),
            (grad_sum, rows_of(rows, width)),
            (weight, all_of(weight.shape)),
            (taps, all_of(taps.shape)),
        ],
        [
            (shaped((tokens, width), BF), rows_of(rows, width)),
            (shaped(weight.shape, BF), all_of(weight.shape)),
            (shaped((8, weight.shape[1]), F32), all_of((8, weight.shape[1]))),
        ],
        [
            pltpu.VMEM((rows + 32, width), F32),
            pltpu.VMEM(weight.shape, F32),
            pltpu.VMEM((rows, weight.shape[1]), BF),
        ],
        4 * tokens * weight.size,
    )


def shifted_from(value, axis, step):
    count = lax.axis_size(axis)
    return lax.ppermute(value, axis, [((i + step) % count, i) for i in range(count)])


def local(
    hidden,
    separators,
    out_grad,
    w_query,
    b_query,
    w_key,
    w_value,
    b_value,
    depth_kernel,
    w_point,
    b_keyconv,
    w_kernel,
    kernel_bias,
    w_convout,
    b_convout,
    w_dense,
    b_dense,
    gain_attn,
    shift_attn,
    w_up,
    b_up,
    w_down,
    b_down,
    gain_out,
    shift_out,
):
    count = lax.axis_size("blk")
    sharers = lax.axis_size("dp")
    me = lax.axis_index("blk")
    x, cotangent = hidden[0], out_grad[0]
    tokens, width = x.shape
    first = me * tokens
    last = count - 1

    others = [shifted_from(x, "blk", step) for step in range(1, count)]
    groups, units = w_up.shape[0], w_up.shape[2]
    columns = jnp.concatenate([w_query, w_key, w_value, w_convout, w_point], axis=1).astype(BF)
    small = jnp.concatenate(
        [v for v in (b_dense, gain_attn, shift_attn, b_down, gain_out, shift_out)]
        + [depth_kernel.T.reshape(-1), b_query, b_value, b_keyconv, b_convout, b_up, w_kernel.reshape(-1)]
    ).astype(BF)
    shard = w_query.shape[0]
    wide = columns.shape[1]
    small_rows = -(-small.size // wide)
    small = jnp.pad(small, (0, small_rows * wide - small.size)).reshape(small_rows, wide)
    early = lax.all_gather(jnp.concatenate([columns, small], axis=0), "dp", axis=0, tiled=False)
    wt_columns = early[:, :shard].reshape(sharers * shard, wide)
    small = early[:, shard:].reshape(sharers, small_rows * wide)
    wt_dense = lax.all_gather(w_dense.astype(BF), "dp", axis=0, tiled=True)
    wt_up = lax.all_gather(
        jnp.concatenate([w_up[g] for g in range(groups)], axis=1).astype(BF), "dp", axis=0, tiled=True
    )
    wt_down = lax.all_gather(
        jnp.concatenate([w_down[g] for g in range(groups)], axis=1).astype(BF), "dp", axis=0, tiled=True
    )
    at = 0
    wide_vectors = small[:, : 15 * shard].reshape(sharers, 15, shard).transpose(1, 0, 2).reshape(15, width).astype(F32)
    at += 15 * shard
    part = b_query.shape[0]
    thin_vectors = small[:, at : at + 4 * part].reshape(sharers, 4, part).transpose(1, 0, 2).reshape(4, ATT).astype(F32)
    at += 4 * part
    bias_up = small[:, at : at + b_up.size].reshape(1, -1).astype(F32)
    at += b_up.size
    wt_kernel = small[:, at : at + w_kernel.size].reshape(ATT, HEADS, KSIZE)
    vectors = jnp.pad(wide_vectors[:6], ((0, 2), (0, 0)))
    taps = jnp.pad(wide_vectors[6:], ((0, 16 - KSIZE), (0, 0)))
    wt_kernel = jnp.pad(wt_kernel.transpose(2, 1, 0), ((0, 0), (0, 8 - HEADS), (0, 0))).reshape(8 * KSIZE, ATT)
    bias_kernel = jnp.pad(kernel_bias.reshape(HEADS, KSIZE).T, ((0, 0), (0, 8 - HEADS))).reshape(8 * KSIZE, 1)
    wt_qkv = wt_columns[:, : 3 * ATT]
    wt_kv = wt_columns[:, ATT : 3 * ATT]
    wt_all = wt_columns[:, : 4 * ATT]
    wt_convout = wt_columns[:, 3 * ATT : 4 * ATT]
    wt_point = wt_columns[:, 4 * ATT :]
    none = jnp.zeros((ATT,), F32)
    bias_kv = jnp.concatenate([none, thin_vectors[1]])[None]
    bias_qkv = jnp.concatenate([thin_vectors[0], none, thin_vectors[1]])[None]

    query, query_t, key, key_t, value, value_t, norms = project(x, wt_qkv, bias_qkv)
    keys = [(key, key_t, value, value_t, norms)]
    outs, probs = [], []
    for step in range(count):
        if step > 0:
            keys.append(project(others[step - 1], wt_kv, bias_kv))
        places = jnp.stack(
            [separators[0], first, lax.rem(me + step, count) * tokens, count * tokens]
        ).astype(jnp.int32)
        out, prob = attend(places, query_t, keys[step][0], keys[step][3], keys[step][4])
        outs.append(out)
        probs.append(prob)
    nothing = jnp.zeros((16, width), BF)
    if count > 1:
        before = jnp.where(me > 0, others[count - 2][tokens - 16 :], nothing)
        after = jnp.where(me < last, others[0][:16], nothing)
    else:
        before = after = nothing
    halo = jnp.concatenate([before, after], axis=0)
    depth, keyconv, attn_key, kernt, kern, conv, values, rim = mix(
        places, x, halo, query, taps, wt_convout, thin_vectors[3][None], wt_point, thin_vectors[2][None], wt_kernel, bias_kernel
    )
    output, grad_sum, grad_conv, grads_t, sides, (gw_dense, gw_up, gw_down, g_vectors, gb_up) = middle(
        outs, conv, x, cotangent, wt_dense, wt_up, wt_down, vectors, bias_up
    )
    packed = jnp.concatenate(
        [
            gw_dense.reshape(sharers, -1, width),
            gw_up.reshape(sharers, -1, width),
            gw_down.reshape(sharers, -1, width),
        ],
        axis=1,
    )
    packed = lax.psum_scatter(packed, "dp", scatter_dimension=0, tiled=False)
    packed = lax.psum(packed, "blk").astype(F32)
    grad_w_dense, grad_w_up, grad_w_down = (
        packed[:shard],
        packed[shard : shard + groups * units * w_up.shape[1] // width],
        packed[-w_down.shape[1] :],
    )
    grad_w_up = grad_w_up.reshape(w_up.shape[1], groups, units).transpose(1, 0, 2)
    grad_w_down = grad_w_down.reshape(w_down.shape[1], groups, -1).transpose(1, 0, 2)

    grad_query_conv, grad_depth, grad_values, gw_point, gw_kernel, g_bias, g_taps = mix_back(
        x, halo, values, rim, grad_conv, kernt, kern, query, keyconv, attn_key, depth, wt_point, wt_kernel
    )
    low_rows = jnp.concatenate([grad_values[:16].astype(BF), grad_depth[:16]], axis=1)
    high_rows = jnp.concatenate([grad_values[tokens + 16 :].astype(BF), grad_depth[tokens - 16 :]], axis=1)
    from_before = lax.ppermute(high_rows, "blk", [(i, i + 1) for i in range(last)])
    from_after = lax.ppermute(low_rows, "blk", [(i + 1, i) for i in range(last)])
    rims = jnp.concatenate([from_before, from_after], axis=0)

    dqs, dks, dvs = [], [], []
    for step in list(range(1, count)) + [0]:
        key, key_t, value, value_t, norms = keys[step]
        dq, dk, dv = attend_back(probs[step], value, key_t, grads_t[step], sides[step], query_t, BF if step else F32)
        if step:
            dk, dv = shifted_from(dk, "blk", count - step), shifted_from(dv, "blk", count - step)
        dqs.append(dq)
        dks.append(dk)
        dvs.append(dv)
    grad_hidden, gw_all, gb_all = finish(
        dqs, dks, dvs, x, grad_query_conv, grad_values, rims[:, :ATT], grad_depth, rims[:, ATT:], grad_sum, wt_all, taps
    )
    gw_kernel, gb_keyconv = (
        gw_kernel[: 8 * KSIZE].reshape(KSIZE, 8, ATT)[:, :HEADS].transpose(2, 1, 0),
        gw_kernel[8 * KSIZE],
    )
    g_bias = g_bias[: 8 * KSIZE, 0].reshape(KSIZE, 8)[:, :HEADS].T.reshape(-1)
    by_device = [
        g_vectors[:6].reshape(6, sharers, shard).transpose(1, 0, 2).reshape(sharers, -1),
        g_taps[:KSIZE].reshape(KSIZE, sharers, shard).transpose(1, 0, 2).reshape(sharers, -1),
        gb_all[0, :ATT].reshape(sharers, -1),
        gb_all[0, 2 * ATT : 3 * ATT].reshape(sharers, -1),
        gb_keyconv.reshape(sharers, -1),
        gb_all[0, 3 * ATT :].reshape(sharers, -1),
        gb_up[0].reshape(sharers, -1),
        gw_kernel.reshape(sharers, -1),
        jnp.broadcast_to(g_bias[None], (sharers, HEADS * KSIZE)),
    ]
    sizes = [v.shape[1] for v in by_device]
    gathered = jnp.concatenate(by_device, axis=1)
    extra_rows = -(-gathered.shape[1] // wide)
    gathered = jnp.pad(gathered, ((0, 0), (0, extra_rows * wide - gathered.shape[1])))
    tail = jnp.concatenate(
        [
            jnp.concatenate([gw_all, gw_point], axis=1).reshape(sharers, shard, wide),
            gathered.astype(BF).reshape(sharers, extra_rows, wide),
        ],
        axis=1,
    )
    tail = lax.psum(lax.psum_scatter(tail, "dp", scatter_dimension=0, tiled=False), "blk").astype(F32)
    gw = [tail[:shard, at * ATT : (at + 1) * ATT] for at in range(5)]
    flat = tail[shard:].reshape(-1)
    ends = [sum(sizes[: at + 1]) for at in range(len(sizes))]
    fields = [flat[end - size : end] for end, size in zip(ends, sizes)]
    grad_vec = fields[0].reshape(6, shard)
    return (
        output[None],
        grad_hidden[None],
        gw[0],
        fields[2],
        gw[1],
        gw[2],
        fields[3],
        fields[1].reshape(KSIZE, shard).T,
        gw[4],
        fields[4],
        fields[7].reshape(w_kernel.shape),
        fields[8],
        gw[3],
        fields[5],
        grad_w_dense,
        grad_vec[0],
        grad_vec[1],
        grad_vec[2],
        grad_w_up,
        fields[6],
        grad_w_down,
        grad_vec[3],
        grad_vec[4],
        grad_vec[5],
    )


def solution(mesh):
    placed = (
        P("dp", "blk", None),
        P("dp"),
        P("dp", "blk", None),
        P("dp", None),
        P("dp"),
        P("dp", None),
        P("dp", None),
        P("dp"),
        P("dp", None),
        P("dp", None),
        P("dp"),
        P("dp", None),
        P(),
        P("dp", None),
        P("dp"),
        P("dp", None),
        P("dp"),
        P("dp"),
        P("dp"),
        P(None, "dp", None),
        P("dp"),
        P(None, "dp", None),
        P("dp"),
        P("dp"),
        P("dp"),
    )
    return jax.shard_map(
        local,
        mesh=mesh,
        in_specs=placed,
        out_specs=(
            P("dp", "blk", None),
            P("dp", "blk", None),
            P("dp", None),
            P("dp"),
            P("dp", None),
            P("dp", None),
            P("dp"),
            P("dp", None),
            P("dp", None),
            P("dp"),
            P("dp", None),
            P(),
            P("dp", None),
            P("dp"),
            P("dp", None),
            P("dp"),
            P("dp"),
            P("dp"),
            P(None, "dp", None),
            P("dp"),
            P(None, "dp", None),
            P("dp"),
            P("dp"),
            P("dp"),
        ),
        check_vma=False,
    )
```

time: 2080 us -> 750 us (0.36)
  matrix products: 916 us -> 0 us
  Pallas kernels: 0 us -> 375 us
  other arithmetic: 344 us -> 30.1 us
  blocking collectives: 271 us -> 0 us
  local copies, waits for them, and re-layouts: 221 us -> 39.1 us
    dot_general x83 -> x0, matrix products: 916 us -> none  [the longest x16 165 us: scored(): jnp.einsum('rqhd,rkhd->rhqk', query_heads, key_heads, preferred_element_t...]
    pallas_call x0 -> x10, Pallas kernels: none -> 375 us  [the longest x6 196 us: run_tiles(): pl.pallas_call(kernel, grid=(steps,), in_specs=list(in_specs), out_specs=...]
    all_gather x7 -> x0, blocking collectives: 141 us -> none  [the longest x1 22.1 us: local(): lax.all_gather(shards[9], 'dp', axis=0, tiled=True)]
    reduce_sum x23 -> x0, other arithmetic: 128 us -> none  [the longest x8 93.2 us: forward_step(): total = total * factor + jnp.sum(weights_now, axis=-1)]
    unnamed x2 -> x0, blocking collectives: 124 us -> none
    unnamed x283 -> x33, local copies, waits for them, and re-layouts: 79.5 us -> 2.75 us
    unnamed x26 -> x8, waiting for transfers between devices: 154 us -> 81.9 us
    dynamic_update_slice x16 -> x0, local copies, waits for them, and re-layouts: 70.1 us -> none  [the longest x8 35.2 us: backward_step(): lax.dynamic_update_slice_in_dim(value_sums, grad_values.reshape(row_count...]
  transfers between devices with their start and end apart: 23 -> 12, of which waited for: 7 -> 5; matrix products, arithmetic and copies ran while one was open for 66% -> 5% of each run, Pallas kernels for 0% -> 22%
where the time goes in v1:
time: 750 us; the launch traced here: 748 us
  Pallas kernels  375 us (50%)
  waiting for transfers between devices  268 us (36%)
  local copies, waits for them, and re-layouts  39.1 us (5%)
  other arithmetic  30.1 us (4%)
  starting transfers between devices  19.2 us (3%)
  between operations  15.6 us (2%)
    pallas_call x6, Pallas kernels, run_tiles(): pl.pallas_call(kernel, grid=(steps,), in_specs=list(in_specs), out_specs=...  196 us
    pallas_call x2, Pallas kernels, attend_back(): pl.pallas_call(functools.partial(attend_back_kernel, keys, queries, chunk...  118 us
    reduce_scatter x1, waiting for transfers between devices, local(): packed = lax.psum_scatter(packed, 'dp', scatter_dimension=0, tiled=False)  85.4 us
    unnamed x8, waiting for transfers between devices  81.9 us
    ppermute x3, waiting for transfers between devices, shifted_from(): lax.ppermute(value, axis, [((i + step) % count, i) for i in range(count)])  64.8 us
    pallas_call x2, Pallas kernels, attend(): pl.pallas_call(functools.partial(attend_kernel, keys, queries, chunk), gr...  61.3 us
    psum x1, waiting for transfers between devices, local(): lax.psum(lax.psum_scatter(tail, 'dp', scatter_dimension=0, tiled=False),...  31.7 us
  transfers between devices with their start and end apart: 12, of which 5 were waited for; matrix products, arithmetic and copies ran while one was open for 5% of the time, Pallas kernels for 22%

profile of v1, /device:TPU:0, one launch (start us, length us, event | category | flops | bytes accessed | tf_op | source)
XLA Modules:
  0.0 747.8 jit_solution(14125370958125739998)
XLA Ops:
  24.9 3.0 collective-permute-start
  31.5 64.8 %collective-permute-done.x_ref = bf16[2048,768]{1,0:T(8,128)(2,1)S(1)} collective-permute-done((bf16[2048,768]{1,0:T(8,128)(2,1)}, bf16[2048,768]{1,0:T(8,128)(2,1)S(1)}, u32[]{:S(2)}, u32[]{:S(2)}) %collective-permute-start) | collective-permute-done | bytes 3145760 | tf_op jit(solution)/shard_map/ppermute | solution.py:738
  102.4 2.0 slice.301
  113.9 12.3 %project.2 = (bf16[2048,384]{1,0:T(8,128)(2,1)}, bf16[384,2048]{1,0:T(8,128)(2,1)}, bf16[2048,384]{1,0:T(8,128)(2,1)}, bf16[384,2048]{1,0:T(8,128)(2,1)}, bf16[2...) custom-call(bf16[2048,768]{1,0:T(8,128)(2,1)} %bitcast.58, bf16[768,1152]{1,0:T(8,128)(2,1)} %slice.302.w_ref, ...), custom_call_target="tpu_custom_call" | custom-call | flops 7247757312 | bytes 14377984 | tf_op jit(solution)/shard_map/project/pallas_call | solution.py:228
  126.2 23.8 %mix.1 = (bf16[2048,768]{1,0:T(8,128)(2,1)}, f32[2048,384]{1,0:T(8,128)}, bf16[2048,384]{1,0:T(8,128)(2,1)}, f32[72,2048]{1,0:T(8,128)}, bf16[2048,128]{1,0:T(8,...) custom-call(s32[4]{0:T(128)} %pad_add_fusion.at_ref, ...), custom_call_target="tpu_custom_call" | custom-call | flops 9663676416 | bytes 18203952 | tf_op jit(solution)/shard_map/mix/pallas_call | solution.py:228
  150.0 8.9 %project.3 = (bf16[2048,384]{1,0:T(8,128)(2,1)}, bf16[384,2048]{1,0:T(8,128)(2,1)}, bf16[2048,384]{1,0:T(8,128)(2,1)}, bf16[384,2048]{1,0:T(8,128)(2,1)}, f32[8,512]{1,0:T(8,128)}) custom-call(bf16[2048,768]{1,0:T(8,128)(2,1)} %copy-done.10, bf16[768,768]{1,0:T(8,128)(2,1)} %slice.307.w_ref, f32[1,768]{1,0:T(1,128)} %broadcast_in_dim.27.bias_ref, ...), custom_call_target="tpu_custom_call" | custom-call | flops 4831838208 | bytes 10639360 | tf_op jit(solution)/shard_map/project/pallas_call | solution.py:228
  158.9 30.6 %attend.3 = (f32[6,80,2048]{2,1,0:T(8,128)}, bf16[6,2048,2048]{2,1,0:T(8,128)(2,1)}) custom-call(s32[4]{0:T(128)} %pad_add_fusion.at_ref, bf16[384,2048]{1,0:T(8,128)(2,1)} %get-tuple-element.76.q_ref, bf16[2048,384]{1,0:T(8,128)(2,1)} %get-tuple-element.81.k_ref, bf16[384,2048]{1,0:T(8,128)(2,1)} %get-tuple-element.82.v_ref, ...), custom_call_target="tpu_custom_call" | custom-call | flops 25769803776 | bytes 50331648 | tf_op jit(solution)/shard_map/attend/pallas_call | solution.py:113
  189.5 30.8 %attend.2 = (f32[6,80,2048]{2,1,0:T(8,128)}, bf16[6,2048,2048]{2,1,0:T(8,128)(2,1)}) custom-call(s32[4]{0:T(128)} %pad_add_fusion.1.at_ref, bf16[384,2048]{1,0:T(8,128)(2,1)} %get-tuple-element.76.q_ref, bf16[2048,384]{1,0:T(8,128)(2,1)} %get-tuple-element.77.k_ref, bf16[384,2048]{1,0:T(8,128)(2,1)} %get-tuple-element.78.v_ref, ...), custom_call_target="tpu_custom_call" | custom-call | flops 25769803776 | bytes 50331648 | tf_op jit(solution)/shard_map/attend/pallas_call | solution.py:113
  220.3 87.3 %middle.1 = (bf16[2048,768]{1,0:T(8,128)(2,1)}, f32[2048,768]{1,0:T(8,128)}, bf16[2048,384]{1,0:T(8,128)(2,1)}, bf16[384,2048]{1,0:T(8,128)(2,1)}, bf16[384,2048...) custom-call(f32[6,80,2048]{2,1,0:T(8,128)} %get-tuple-element.80.ref, ...), custom_call_target="tpu_custom_call" | custom-call | flops 36238786560 | bytes 42627072 | tf_op jit(solution)/shard_map/middle/pallas_call | solution.py:228
  307.6 35.5 %mix_back.1 = (f32[2048,384]{1,0:T(8,128)}, bf16[2048,768]{1,0:T(8,128)(2,1)}, f32[2080,384]{1,0:T(8,128)}, bf16[768,384]{1,0:T(8,128)(2,1)}, f32[80,384]{1,0:T(...) custom-call(bf16[2048,768]{1,0:T(8,128)(2,1)} %bitcast.61, bf16[32,768]{1,0:T(8,128)(2,1)} %pad_maximum_fusion.5.halo_ref, ...), custom_call_target="tpu_custom_call" | custom-call | flops 9663676416 | bytes 27850752 | tf_op jit(solution)/shard_map/mix_back/pallas_call | solution.py:228
  343.9 58.7 %attend_back.2 = (f32[384,2048]{1,0:T(8,128)}, bf16[384,2048]{1,0:T(8,128)(2,1)}, bf16[384,2048]{1,0:T(8,128)(2,1)}) custom-call(bf16[6,2048,2048]{2,1,0:T(8,128)(2,1)} %get-tuple-element.88.p_ref, bf16[2048,384]{1,0:T(8,128)(2,1)} %get-tuple-element.89.v_ref, bf16[384,2048]{1,0:T(8,128)(2,1)} %get-tuple-element.90.kt_ref, ...), custom_call_target="tpu_custom_call" | custom-call | flops 51539607552 | bytes 50331648 | tf_op jit(solution)/shard_map/attend_back/pallas_call | solution.py:179
  402.6 10.7 %collective-permute-start.1 = (bf16[384,2048]{1,0:T(8,128)(2,1)}, bf16[384,2048]{1,0:T(8,128)(2,1)}, u32[]{:S(2)}, u32[]{:S(2)}) collective-permute-start(bf16[384,2048]{1,0:T(8,128)(2,1)} %get-tuple-element.100), channel_id=1, source_target_pairs={{16,0},{0,16},{17,1},{1,17},{18,2},{2,18},{19,3},{3,19},{20,4},{4,... | collective-permute-start | bytes 4718600 | tf_op jit(solution)/shard_map/ppermute | solution.py:738
  413.6 3.9 collective-permute-start.3
  417.5 59.1 %attend_back.3 = (f32[384,2048]{1,0:T(8,128)}, f32[384,2048]{1,0:T(8,128)}, f32[384,2048]{1,0:T(8,128)}) custom-call(bf16[6,2048,2048]{2,1,0:T(8,128)(2,1)} %get-tuple-element.94.p_ref, bf16[2048,384]{1,0:T(8,128)(2,1)} %get-tuple-element.95.v_ref, bf16[384,2048]{1,0:T(8,128)(2,1)} %get-tuple-element.96.kt_ref, bf16[384,2048]{1,0:T(8,128)(2,1)} %get-tuple-element.97.g_ref, ...), custom_call_target="tpu_custom_call" | custom-call | flops 51539607552 | bytes 50331648 | tf_op jit(solution)/shard_map/attend_back/pallas_call | solution.py:179
  477.8 1.6 slice.327.refs_13_
  482.8 4.5 collective-permute-done.4
  488.6 28.6 %finish.1 = (bf16[2048,768]{1,0:T(8,128)(2,1)}, bf16[768,1536]{1,0:T(8,128)(2,1)}, f32[8,1536]{1,0:T(8,128)}) custom-call(f32[384,2048]{1,0:T(8,128)} %get-tuple-element.93.refs_0_, f32[384,2048]{1,0:T(8,128)} %get-tuple-element.99.refs_1_, bf16[384,2048]{1,0:T(8,128)(2,1)} %collective-permute-done.1.refs_2_, f32[384,2048]{1,0:T(8,128)} %get-tuple-element.101.refs_3_, ...), custom_call_target="tpu_custom_call" | custom-call | flops 9663676416 | bytes 42688512 | tf_op jit(solution)/shard_map/finish/pallas_call | solution.py:228
  518.5 1.9 pad_maximum_fusion.2
  520.4 2.1 pad_maximum_fusion.1
  522.6 3.9 reshape.201
  526.5 4.6 pad_maximum_fusion
  531.2 81.8 %reduce-scatter.7.cloned.1.call-done = bf16[1,50,1920]{2,1,0:T(8,128)(2,1)} async-done(((bf16[16,50,1920]{2,1,0:T(8,128)(2,1)}), bf16[1,50,1920]{2,1,0:T(8,128)(2,1)}) %reduce-scatter.7.cloned.1.call-update) | async-done | bytes 192016
  613.0 85.4 %reduce-scatter.5.cloned.1.call-done = bf16[1,240,768]{2,1,0:T(8,128)(2,1)} async-done(((bf16[16,240,768]{2,1,0:T(8,128)(2,1)}), bf16[1,240,768]{2,1,0:T(8,128)(2,1)}) %reduce-scatter.5.cloned.1.call-update) | async-done | bytes 368656 | tf_op jit(solution)/shard_map/reduce_scatter | solution.py:852
  698.4 31.7 %all-reduce.10.cloned.1.call-done = (bf16[50,1920]{1,0:T(8,128)(2,1)}, bf16[240,768]{1,0:T(8,128)(2,1)}) async-done(((bf16[50,1920]{1,0:T(8,128)(2,1)}, bf16[240,768]{1,0:T(8,128)(2,1)}), (bf16[50,1920]{1,0:T(8,128)(2,1)}, bf16[240,768]{1,0:T(8,128)(2,1)})) %all-reduce.10.cloned.1.call-update) | async-done | bytes 560656 | tf_op jit(solution)/shard_map/psum | solution.py:910
  (180 shorter events, 54.8 us)
Async XLA Ops:
  7.2 20.8 %copy-start.5 = (f32[2,96,384]{2,1,0:T(8,128)S(1)}, f32[2,96,384]{2,1,0:T(8,128)}, u32[]{:S(2)}) copy-start(f32[2,96,384]{2,1,0:T(8,128)} %param.46) | copy-start | bytes 884740
  7.2 22.2 %copy-start.12 = (f32[54]{0:T(128)S(1)}, f32[54]{0:T(128)}, u32[]{:S(2)}) copy-start(f32[54]{0:T(128)} %param.37) | copy-start | bytes 652
  7.2 89.8 %all-gather.13.cloned.1.call-start = ((), (), s32[]{:S(2)}) async-start(), calls=%async_computation.6 | async-start | bytes 3655680 | tf_op jit(solution)/shard_map/all_gather | solution.py:787
  21.5 198.8 %all-gather.7.cloned.1.call-start = ((), (), s32[]{:S(2)}) async-start(), calls=%async_computation.2 | async-start | bytes 1253376 | tf_op jit(solution)/shard_map/all_gather | solution.py:790
  23.1 197.2 %all-gather.9.cloned.1.call-start = ((), (), s32[]{:S(2)}) async-start(), calls=%async_computation.3 | async-start | bytes 2506752 | tf_op jit(solution)/shard_map/all_gather | solution.py:791
  24.9 195.4 %all-gather.11.cloned.1.call-start = ((), (), s32[]{:S(2)}) async-start(), calls=%async_computation.4 | async-start | bytes 2506752 | tf_op jit(solution)/shard_map/all_gather | solution.py:794
  24.9 71.3 %collective-permute-start = (bf16[2048,768]{1,0:T(8,128)(2,1)}, bf16[2048,768]{1,0:T(8,128)(2,1)S(1)}, u32[]{:S(2)}, u32[]{:S(2)}) collective-permute-start(bf16[2048,768]{1,0:T(8,128)(2,1)} %bitcast.57), channel_id=1, source_target_pairs={{16,0},{0,16},{17,1},{1,17},{18,2},{2,18},{19,3},{3,19},{20,4},{4,... | collective-permute-start | bytes 9437192 | tf_op jit(solution)/shard_map/ppermute | solution.py:738
  28.7 584.3 %reduce-scatter.7.cloned.1.call-start = ((), (), s32[]{:S(2)}) async-start(), calls=%async_computation.7 | async-start | bytes 3655680
  104.4 2.4 copy-start
  106.8 6.4 copy-start.11
  343.9 69.5 %copy-start.2 = (f32[2080,384]{1,0:T(8,128)S(1)}, f32[2080,384]{1,0:T(8,128)}, u32[]{:S(2)}) copy-start(f32[2080,384]{1,0:T(8,128)} %get-tuple-element.113.refs_8_) | copy-start | bytes 9584644
  402.6 86.0 %collective-permute-start.1 = (bf16[384,2048]{1,0:T(8,128)(2,1)}, bf16[384,2048]{1,0:T(8,128)(2,1)}, u32[]{:S(2)}, u32[]{:S(2)}) collective-permute-start(bf16[384,2048]{1,0:T(8,128)(2,1)} %get-tuple-element.100), channel_id=1, source_target_pairs={{16,0},{0,16},{17,1},{1,17},{18,2},{2,18},{19,3},{3,19},{20,4},{4,... | collective-permute-start | bytes 4718600 | tf_op jit(solution)/shard_map/ppermute | solution.py:738
  413.3 75.3 %collective-permute-start.2 = (bf16[384,2048]{1,0:T(8,128)(2,1)}, bf16[384,2048]{1,0:T(8,128)(2,1)}, u32[]{:S(2)}, u32[]{:S(2)}) collective-permute-start(bf16[384,2048]{1,0:T(8,128)(2,1)} %get-tuple-element.102), channel_id=1, source_target_pairs={{16,0},{0,16},{17,1},{1,17},{18,2},{2,18},{19,3},{3,19},{20,4},{4,... | collective-permute-start | bytes 4718600 | tf_op jit(solution)/shard_map/ppermute | solution.py:738
  413.6 69.2 %collective-permute-start.3 = (bf16[16,1152]{1,0:T(8,128)(2,1)S(1)}, bf16[16,1152]{1,0:T(8,128)(2,1)S(1)}, u32[]{:S(2)}, u32[]{:S(2)}) collective-permute-start(bf16[16,1152]{1,0:T(8,128)(2,1)S(1)} %pad_maximum_fusion.6), channel_id=1, source_target_pairs={{0,16},{1,17},{2,18},{3,19},{4,20},{5,21},{6,22},{7,23},{8,24},{9,... | collective-permute-start | bytes 110600 | tf_op jit(solution)/shard_map/ppermute | solution.py:867
  417.4 59.1 %copy-start.7 = (f32[80,128]{1,0:T(8,128)S(1)}, f32[80,128]{1,0:T(8,128)}, u32[]{:S(2)}) copy-start(f32[80,128]{1,0:T(8,128)} %get-tuple-element.124) | copy-start | bytes 122884
  417.5 59.3 %copy-start.6 = (f32[80,384]{1,0:T(8,128)S(1)}, f32[80,384]{1,0:T(8,128)}, u32[]{:S(2)}) copy-start(f32[80,384]{1,0:T(8,128)} %get-tuple-element.122) | copy-start | bytes 368644
  417.5 60.3 %copy-start.1 = (bf16[16,48,1920]{2,1,0:T(8,128)(2,1)S(1)}, bf16[16,48,1920]{2,1,0:T(8,128)(2,1)}, u32[]{:S(2)}) copy-start(bf16[16,48,1920]{2,1,0:T(8,128)(2,1)} %copy-done) | copy-start | bytes 8847364
  476.6 3.1 copy-start.9
  476.6 3.3 copy-start.8
  481.5 5.8 collective-permute-start.4
  488.6 29.9 %copy-start.4 = (bf16[768,384]{1,0:T(8,128)(2,1)S(1)}, bf16[768,384]{1,0:T(8,128)(2,1)}, u32[]{:S(2)}) copy-start(bf16[768,384]{1,0:T(8,128)(2,1)} %get-tuple-element.118) | copy-start | bytes 1769476
  522.5 4.0 copy-start.3
  522.5 175.8 %reduce-scatter.5.cloned.1.call-start = ((), (), s32[]{:S(2)}) async-start(), calls=%async_computation.5 | async-start | bytes 6266880 | tf_op jit(solution)/shard_map/reduce_scatter | solution.py:852
  531.2 199.0 %all-reduce.10.cloned.1.call-start = ((), (), s32[]{:S(2)}) async-start(), calls=%async_computation.8 | async-start | bytes 1167360 | tf_op jit(solution)/shard_map/psum | solution.py:910
  (1 other events, 2.2 us)
Sparse Core Ops, SparseCore 0:
  21.6 49.3 all-gather.12
  73.9 37.2 all-gather.6
  114.1 41.1 all-gather.8
  158.0 41.0 all-gather.10
  522.6 90.2 reduce-scatter.6
  616.8 81.5 reduce-scatter.4
  700.9 29.1 all-reduce.9
